TPU v7x, 1024 devices: a whole 4x4x32 slice. The times are simulated.
1024 devices in a mesh: dp: 4 (over y), fsdp: 64 (over z, core), tensor: 4 (over x).
Axes of the slice: x: 4, y: 4, z: 32, core: 2. Of those that a mesh axis runs over, the one named last changes fastest.
Arguments:
- momentum: bfloat16 [4, 14336, 8192], P('dp', 'fsdp', 'tensor'), may hold values from -6 to 6
- gradient: bfloat16 [4, 14336, 8192], P('dp', 'fsdp', 'tensor'), may hold values from -100 to 100, as said below
- basis: float32 [256, 8192], P('fsdp', 'tensor'), may hold values from -0.0625 to 0.0625
Outputs:
- momentum_next: bfloat16 [4, 14336, 8192], P('dp', 'fsdp', 'tensor')
- update: bfloat16 [14336, 8192], P('fsdp', 'tensor')
- basis_next: float32 [256, 8192], P('fsdp', 'tensor')
Inputs may be any that keep to these rules, and one draw needn't show every extreme that they name: Row and column scales of each replica's gradient vary.
All inputs are finite; a program needn't handle non-finite values.
Results may differ from a plain program's by a relative error of at most 0.027.
Values may be sent and summed in bfloat16 or wider, within the bound.
No kernel may reach another device: no remote copies, remote signals or barrier semaphores. Data moves between devices by JAX's collectives and lax.ppermute only.
A program may use at most 32 MiB of HBM per device.

v0:
```python
import jax
import jax.numpy as jnp
from jax import lax
from jax.sharding import PartitionSpec as P

D = 8192
FF = 14336
RANK = 256


epsilon = 1e-06


def body(momentum, gradient, basis):
    replicas = lax.axis_size("dp")
    buffer = momentum[0].astype(jnp.float32) + gradient[0].astype(jnp.float32)
    buffer_h = buffer.astype(jnp.bfloat16)
    left_term = lax.dot_general(
        buffer_h,
        lax.all_gather(basis.astype(jnp.bfloat16), "fsdp", axis=0, tiled=True),
        (((1,), (1,)), ((), ())),
        preferred_element_type=jnp.float32,
    )
    left_full = (
        lax.psum(left_term.astype(jnp.bfloat16), ("dp", "tensor")).astype(jnp.float32) / replicas
    )
    left_squares = lax.psum(jnp.sum(left_full * left_full, axis=0), "fsdp")
    left_hat = (left_full / jnp.sqrt(left_squares + epsilon)[None, :]).astype(jnp.bfloat16)
    own_count = basis.shape[0]
    right_piece = lax.psum_scatter(
        lax.dot_general(
            left_hat, buffer_h, (((0,), (0,)), ((), ())), preferred_element_type=jnp.float32
        ),
        "fsdp",
        scatter_dimension=0,
        tiled=True,
    )
    right_piece = lax.psum(right_piece.astype(jnp.bfloat16), "dp").astype(jnp.float32) / replicas
    right_h = lax.all_gather(right_piece.astype(jnp.bfloat16), "fsdp", axis=0, tiled=True)
    right_wide = right_h.astype(jnp.float32)
    right_squares = lax.psum(jnp.sum(right_wide * right_wide, axis=1), "tensor")
    next_full = right_wide / jnp.sqrt(right_squares + epsilon)[:, None]
    basis_next = lax.dynamic_slice_in_dim(
        next_full, lax.axis_index("fsdp") * own_count, own_count, 0
    )
    scale = (FF * D / RANK) ** 0.5
    update = (
        jnp.dot(left_hat, next_full.astype(jnp.bfloat16), preferred_element_type=jnp.float32)
        * scale
    ).astype(jnp.bfloat16)
    feedback = jnp.dot(left_hat, right_h, preferred_element_type=jnp.float32)
    momentum_next = (buffer - 0.05 * feedback).astype(jnp.bfloat16)[None]
    return (momentum_next, update, basis_next)


def solution(mesh):
    return jax.shard_map(
        body,
        mesh=mesh,
        in_specs=(P("dp", "fsdp", "tensor"), P("dp", "fsdp", "tensor"), P("fsdp", "tensor")),
        out_specs=(P("dp", "fsdp", "tensor"), P("fsdp", "tensor"), P("fsdp", "tensor")),
        check_vma=False,
    )
```

profile of v0, /device:TPU:1, one launch (start us, length us, event | category | flops | bytes accessed | tf_op | source)
XLA Modules:
  0.0 769.0 jit_solution(2955300760944769924)
XLA Ops:
  7.2 0.0 copy-start.1
  7.2 0.0 copy-start
  7.2 0.0 all-gather.5.cloned.1.call-start
  7.2 1.5 convert_bitcast_fusion
  8.7 0.0 all-gather.5.cloned.1.call-update
  8.7 0.0 all-reduce.4.cloned.1.call-start
  8.8 146.6 %all-gather.5.cloned.1.call-done = bf16[64,4,2048]{2,1,0:T(4,128)(2,1)} async-done(((bf16[1,4,2048]{2,1,0:T(4,128)(2,1)}), bf16[64,4,2048]{2,1,0:T(4,128)(2,1)}) %all-gather.5.cloned.1.call-update) | async-done | bytes 1048592 | tf_op jit(solution)/shard_map/all_gather | solution.py:20
  155.4 1.3 reshape.12
  156.8 0.0 copy-done.1
  156.8 0.0 copy-done
  156.8 1.2 convolution_convert_fusion
  157.9 0.0 all-reduce.4.cloned.1.call-update
  158.0 0.0 all-gather.7.cloned.1.call-start
  158.0 1.3 dynamic-slice
  159.9 142.6 %all-reduce.4.cloned.1.call-done = bf16[224,256]{1,0:T(8,128)(2,1)} async-done(((bf16[224,256]{1,0:T(8,128)(2,1)}), bf16[224,256]{1,0:T(8,128)(2,1)}) %all-reduce.4.cloned.1.call-update) | async-done | bytes 114704 | tf_op jit(solution)/shard_map/psum | solution.py:25
  302.5 1.0 multiply_reduce_fusion
  303.5 94.8 %psum.29 = f32[256]{0:T(256)S(1)} all-reduce(f32[256]{0:T(256)S(1)} %multiply_reduce_fusion), channel_id=1, replica_groups=mesh['dp'=4,'fsdp'=64,'tensor'=4] {'fsdp'}, use_global_device_ids=true, to_apply=%region_2.0 | all-reduce | flops 256 | bytes 2048 | tf_op jit(solution)/shard_map/psum | solution.py:27
  398.3 1.7 fusion.6
  400.0 197.2 %all-reduce.5 = bf16[256,2048]{1,0:T(8,128)(2,1)} all-reduce(f32[256,2048]{1,0:T(8,128)S(1)} %fusion.6), channel_id=2, replica_groups=mesh['dp'=4,'fsdp'=64,'tensor'=4] {'fsdp'}, use_global_device_ids=true, to_apply=%region_3.0.clone | all-reduce | flops 524288 | bytes 3145728
  597.2 0.8 dynamic-slice_convert_fusion
  598.0 11.8 %psum.30 = bf16[4,2048]{1,0:T(4,128)(2,1)S(1)} all-reduce(bf16[4,2048]{1,0:T(4,128)(2,1)S(1)} %dynamic-slice_convert_fusion), channel_id=1, replica_groups=mesh['dp'=4,'fsdp'=64,'tensor'=4] {'dp'}, use_global_device_ids=true, to_apply=%region_4.0 | all-reduce | flops 8192 | bytes 32768 | tf_op jit(solution)/shard_map/psum | solution.py:38
  609.8 0.6 fusion.7
  610.4 0.0 all-gather.7.cloned.1.call-update
  610.5 138.0 %all-gather.7.cloned.1.call-done = bf16[64,4,2048]{2,1,0:T(4,128)(2,1)} async-done(((bf16[1,4,2048]{2,1,0:T(4,128)(2,1)}), bf16[64,4,2048]{2,1,0:T(4,128)(2,1)}) %all-gather.7.cloned.1.call-update) | async-done | bytes 1048592 | tf_op jit(solution)/shard_map/all_gather | solution.py:39
  748.5 1.3 reshape.14
  749.8 0.3 fusion.4
  750.1 0.0 copy-start.3
  750.1 8.5 %psum.31 = f32[256]{0:T(256)S(1)} all-reduce(f32[256]{0:T(256)S(1)} %fusion.4), channel_id=1, replica_groups=mesh['dp'=4,'fsdp'=64,'tensor'=4] {'tensor'}, use_global_device_ids=true, to_apply=%region_6.0 | all-reduce | flops 256 | bytes 2048 | tf_op jit(solution)/shard_map/psum | solution.py:41
  758.7 0.3 convert_divide_fusion
  758.9 0.6 constant_dynamic-slice_fusion
  759.6 0.0 copy-done.3
  759.6 0.0 copy-start.2
  759.6 1.4 fusion.2
  761.0 0.0 copy-done.2
  761.0 1.4 fusion.3
  (2 shorter events, 0.0 us)
Async XLA Ops:
  7.2 149.6 %copy-start.1 = (bf16[1,224,2048]{2,1,0:T(8,128)(2,1)S(1)}, bf16[1,224,2048]{2,1,0:T(8,128)(2,1)}, u32[]{:S(2)}) copy-start(bf16[1,224,2048]{2,1,0:T(8,128)(2,1)} %param.3) | copy-start | bytes 2752516
  7.2 149.6 %copy-start = (bf16[1,224,2048]{2,1,0:T(8,128)(2,1)S(1)}, bf16[1,224,2048]{2,1,0:T(8,128)(2,1)}, u32[]{:S(2)}) copy-start(bf16[1,224,2048]{2,1,0:T(8,128)(2,1)} %param.4) | copy-start | bytes 2752516
  7.2 148.2 %all-gather.5.cloned.1.call-start = ((), (), s32[]{:S(2)}) async-start(), calls=%async_computation.1 | async-start | bytes 1064960 | tf_op jit(solution)/shard_map/all_gather | solution.py:20
  8.7 293.8 %all-reduce.4.cloned.1.call-start = ((), (), s32[]{:S(2)}) async-start(), calls=%async_computation | async-start | bytes 229376 | tf_op jit(solution)/shard_map/psum | solution.py:25
  158.0 590.5 %all-gather.7.cloned.1.call-start = ((), (), s32[]{:S(2)}) async-start(), calls=%async_computation.2 | async-start | bytes 1064960 | tf_op jit(solution)/shard_map/all_gather | solution.py:39
  750.1 9.5 %copy-start.3 = (bf16[224,256]{1,0:T(8,128)(2,1)S(1)}, bf16[224,256]{1,0:T(8,128)(2,1)}, u32[]{:S(2)}) copy-start(bf16[224,256]{1,0:T(8,128)(2,1)} %all-reduce.4.cloned.1.call-done) | copy-start | bytes 344068
  759.6 1.5 copy-start.2
Sparse Core Ops, SparseCore 0:
  11.3 144.0 all-gather.4
  159.2 143.2 all-reduce.3
  610.6 137.8 all-gather.6
where the time goes:
time: 770 us; the launch traced here: 769 us
  waiting for transfers between devices  427 us (55%)
  blocking collectives  312 us (41%)
  between operations  14.5 us (2%)
    unnamed x1, blocking collectives  197 us
    all_gather x1, waiting for transfers between devices, body(): lax.all_gather(basis.astype(jnp.bfloat16), 'fsdp', axis=0, tiled=True)  147 us
    psum x1, waiting for transfers between devices, body(): lax.psum(left_term.astype(jnp.bfloat16), ('dp', 'tensor'))  143 us
    all_gather x1, waiting for transfers between devices, body(): lax.all_gather(right_piece.astype(jnp.bfloat16), 'fsdp', axis=0, tiled=True)  138 us
    psum x1, blocking collectives, body(): left_squares = lax.psum(jnp.sum(left_full * left_full, axis=0), 'fsdp')  94.8 us
  transfers between devices with their start and end apart: 3, of which 3 were waited for; matrix products, arithmetic and copies ran while one was open for 0% of the time, Pallas kernels for 0%

commit v1 on v0

v1 whole, which is shorter than its diff:
```python
import jax
import jax.numpy as jnp
from jax import lax
from jax.sharding import Mesh, PartitionSpec as P

D = 8192
FF = 14336
RANK = 256

epsilon = 1e-06
f32 = jnp.float32
bf16 = jnp.bfloat16

NEAR = ("zl", "core")
PLANE = ("dp", "tensor")


def exchange(blocks, axes):
    return lax.all_to_all(blocks, axes, 0, 0, tiled=False)


def gather(block, axes):
    count = lax.axis_size(axes)
    return exchange(jnp.broadcast_to(block[None], (count,) + block.shape), axes)


def pair_lanes(values):
    high = lax.reduce_precision(values, 8, 7)
    low = (values - high).astype(bf16)
    high = high.astype(bf16)
    rows = values.shape[0]
    return jnp.concatenate(
        [jnp.broadcast_to(high[:, None], (rows, 64)), jnp.broadcast_to(low[:, None], (rows, 64))], axis=1
    )


def from_lanes(lanes):
    return lanes[..., 0].astype(f32) + lanes[..., 64].astype(f32)


def body(momentum, gradient, basis):
    replicas = lax.axis_size("dp")
    far = lax.axis_size("zh")
    near = lax.axis_size(NEAR)
    plane = lax.axis_size(PLANE)
    me = lax.axis_index("dp")
    own_rows, width = basis.shape
    part = width // replicas
    rank = own_rows * far * near

    own_basis = lax.dynamic_slice_in_dim(basis, me * part, part, 1).astype(bf16)
    far_basis = gather(own_basis, "zh").reshape(far * own_rows, part)

    def column_block(index):
        first = lax.dynamic_slice_in_dim(momentum[0], index * part, part, 1).astype(f32)
        second = lax.dynamic_slice_in_dim(gradient[0], index * part, part, 1).astype(f32)
        return (first + second).astype(bf16)

    pieces = [
        lax.ppermute(
            column_block((me + k) % replicas), "dp", [(i, (i + k) % replicas) for i in range(replicas)]
        )
        for k in range(1, replicas)
    ]
    far_basis, *pieces = lax.optimization_barrier((far_basis, *pieces))
    basis_h = gather(far_basis, NEAR).reshape(rank, part)
    total = column_block(me).astype(f32)
    for piece in pieces:
        total = total + piece.astype(f32)
    mean_h = (total / replicas).astype(bf16)

    left_term = lax.dot_general(
        basis_h, mean_h, (((1,), (1,)), ((), ())), preferred_element_type=f32
    ).astype(bf16)
    ff = left_term.shape[1]
    left_own = jnp.sum(
        exchange(left_term.reshape(plane, rank // plane, ff), PLANE).astype(f32), axis=0
    )
    left_t = gather(left_own.astype(bf16), PLANE).reshape(rank, ff)
    left_wide = left_t.astype(f32)
    squares = jnp.sum(left_wide * left_wide, axis=1)

    right_term = jnp.dot(left_t, mean_h, preferred_element_type=f32).astype(bf16)
    packed = jnp.concatenate([right_term, pair_lanes(squares)], axis=1)
    packed = exchange(packed.reshape(near, rank // near, part + 128), NEAR)
    right_near = jnp.sum(packed[..., :part].astype(f32), axis=0)
    squares_near = jnp.sum(from_lanes(packed[..., part:]), axis=0)
    packed = jnp.concatenate([right_near.astype(bf16), pair_lanes(squares_near)], axis=1)
    packed = exchange(packed.reshape(far, own_rows, part + 128), "zh")
    right_un = jnp.sum(packed[..., :part].astype(f32), axis=0)
    norms = jnp.sqrt(jnp.sum(from_lanes(packed[..., part:]), axis=0) + epsilon)
    right_own = (right_un / norms[:, None]).astype(bf16)

    packed = jnp.concatenate([right_own, pair_lanes(norms)], axis=1)
    packed = gather(packed, "zh").reshape(far * own_rows, part + 128)
    packed = gather(packed, ("dp",) + NEAR).reshape(replicas, rank, part + 128)
    right_h = packed[..., :part]
    norms_all = from_lanes(packed[0, :, part:])
    left_hat = (left_wide / norms_all[:, None]).astype(bf16)
    right_wide = right_h.astype(f32)
    right_squares = lax.psum(jnp.sum(right_wide * right_wide, axis=(0, 2)), "tensor")
    right_norms = jnp.sqrt(right_squares + epsilon)
    next_h = (right_wide / right_norms[None, :, None]).astype(bf16)

    row = (lax.axis_index(NEAR) * far + lax.axis_index("zh")) * own_rows
    own_right = lax.dynamic_slice_in_dim(right_h, row, own_rows, 1).astype(f32)
    own_norms = lax.dynamic_slice_in_dim(right_norms, row, own_rows, 0)
    basis_next = (own_right / own_norms[None, :, None]).transpose(1, 0, 2).reshape(own_rows, width)

    scale = (FF * D / RANK) ** 0.5
    update, momentum_next = [], []
    for d in range(replicas):
        def product(right):
            return lax.dot_general(
                left_hat, right, (((0,), (0,)), ((), ())), preferred_element_type=f32
            )

        columns = slice(d * part, (d + 1) * part)
        buffer = momentum[0, :, columns].astype(f32) + gradient[0, :, columns].astype(f32)
        momentum_next.append((buffer - 0.05 * product(right_h[d])).astype(bf16))
        update.append((product(next_h[d]) * scale).astype(bf16))
    return (
        jnp.concatenate(momentum_next, axis=1)[None],
        jnp.concatenate(update, axis=1),
        basis_next,
    )


def solution(mesh):
    replicas, fsdp, tensor = (mesh.shape[name] for name in ("dp", "fsdp", "tensor"))
    fine = Mesh(
        mesh.devices.reshape(replicas, fsdp // 4, 2, 2, tensor), ("dp", "zh", "zl", "core", "tensor")
    )
    z = ("zh", "zl", "core")
    return jax.shard_map(
        body,
        mesh=fine,
        in_specs=(P("dp", z, "tensor"), P("dp", z, "tensor"), P(z, "tensor")),
        out_specs=(P("dp", z, "tensor"), P(z, "tensor"), P(z, "tensor")),
        check_vma=False,
    )
```

time: 770 us -> 214 us (0.28)
  waiting for transfers between devices: 427 us -> 31.9 us
  blocking collectives: 312 us -> 108 us
  starting transfers between devices: 0.12 us -> 54.5 us
  between operations: 14.5 us -> 0.98 us
    all_gather x2 -> x0, waiting for transfers between devices: 285 us -> none  [the longest x1 147 us: body(): lax.all_gather(basis.astype(jnp.bfloat16), 'fsdp', axis=0, tiled=True)]
    unnamed x1 -> x0, blocking collectives: 197 us -> none
    psum x1 -> x0, waiting for transfers between devices: 143 us -> none  [body(): lax.psum(left_term.astype(jnp.bfloat16), ('dp', 'tensor'))]
    psum x3 -> x1, blocking collectives: 115 us -> 6.65 us  [body(): lax.psum(jnp.sum(right_wide * right_wide, axis=(0, 2)), 'tensor')]
    all_to_all x0 -> x5, blocking collectives: none -> 101 us  [exchange(): return lax.all_to_all(blocks, axes, 0, 0, tiled=False)]
    all_to_all x0 -> x3, starting transfers between devices: none -> 43.8 us  [exchange(): return lax.all_to_all(blocks, axes, 0, 0, tiled=False)]
    all_to_all x0 -> x3, waiting for transfers between devices: none -> 31.9 us  [exchange(): return lax.all_to_all(blocks, axes, 0, 0, tiled=False)]
    ppermute x0 -> x3, starting transfers between devices: none -> 10.7 us  [body(): lax.ppermute(column_block((me + k) % replicas), 'dp', [(i, (i + k) % repl...]
  transfers between devices with their start and end apart: 3 -> 6, of which waited for: 3 -> 3; matrix products, arithmetic and copies ran while one was open for 0% -> 1% of each run, Pallas kernels for 0% -> 0%
where the time goes in v1:
time: 214 us; the launch traced here: 213 us
  blocking collectives  108 us (50%)
  starting transfers between devices  54.5 us (25%)
  waiting for transfers between devices  31.9 us (15%)
  other arithmetic  8.37 us (4%)
  local copies, waits for them, and re-layouts  4.74 us (2%)
  matrix products  4.42 us (2%)
    all_to_all x5, blocking collectives, exchange(): return lax.all_to_all(blocks, axes, 0, 0, tiled=False)  101 us
    all_to_all x3, starting transfers between devices, exchange(): return lax.all_to_all(blocks, axes, 0, 0, tiled=False)  43.8 us
    all_to_all x3, waiting for transfers between devices, exchange(): return lax.all_to_all(blocks, axes, 0, 0, tiled=False)  31.9 us
    ppermute x3, starting transfers between devices, body(): lax.ppermute(column_block((me + k) % replicas), 'dp', [(i, (i + k) % repl...  10.7 us
    psum x1, blocking collectives, body(): lax.psum(jnp.sum(right_wide * right_wide, axis=(0, 2)), 'tensor')  6.65 us
  transfers between devices with their start and end apart: 6, of which 3 were waited for; matrix products, arithmetic and copies ran while one was open for 1% of the time, Pallas kernels for 0%

profile of v1, /device:TPU:1, one launch (start us, length us, event | category | flops | bytes accessed | tf_op | source)
XLA Modules:
  0.0 212.6 jit_solution(14482536370756981887)
XLA Ops:
  0.7 0.7 copy-done
  1.4 0.7 broadcast_in_dim.26
  2.1 29.0 %all-to-all-start = ((bf16[16,4,512]{2,1,0:T(4,128)(2,1)}), bf16[16,4,512]{2,1,0:T(4,128)(2,1)S(1)}, u32[]{:S(2)}, u32[]{:S(2)}) async-start(bf16[16,4,512]{2,1,0:T(4,128)(2,1)} %broadcast_in_dim.26), calls=%async_computation | async-start | bytes 131072 | tf_op jit(solution)/shard_map/all_to_all | solution.py:19
  31.1 1.7 fusion.22
  32.8 3.2 %collective-permute-start = (bf16[224,512]{1,0:T(8,128)(2,1)S(1)}, bf16[224,512]{1,0:T(8,128)(2,1)S(1)}, u32[]{:S(2)}, u32[]{:S(2)}) collective-permute-start(bf16[224,512]{1,0:T(8,128)(2,1)S(1)} %get-tuple-element.13), channel_id=1, source_target_pairs={{0,256},{256,512},{512,768},{768,0},{1,257},{257,513},{513,769},{7... | collective-permute-start | bytes 688136 | tf_op jit(solution)/shard_map/ppermute | solution.py:60
  36.0 4.5 %collective-permute-start.1 = (bf16[224,512]{1,0:T(8,128)(2,1)S(1)}, bf16[224,512]{1,0:T(8,128)(2,1)S(1)}, u32[]{:S(2)}, u32[]{:S(2)}) collective-permute-start(bf16[224,512]{1,0:T(8,128)(2,1)S(1)} %get-tuple-element.12), channel_id=1, source_target_pairs={{0,512},{256,768},{512,0},{768,256},{1,513},{257,769},{513,1},{769... | collective-permute-start | bytes 688136 | tf_op jit(solution)/shard_map/ppermute | solution.py:60
  40.5 3.0 %collective-permute-start.2 = (bf16[224,512]{1,0:T(8,128)(2,1)S(1)}, bf16[224,512]{1,0:T(8,128)(2,1)S(1)}, u32[]{:S(2)}, u32[]{:S(2)}) collective-permute-start(bf16[224,512]{1,0:T(8,128)(2,1)S(1)} %get-tuple-element.11), channel_id=1, source_target_pairs={{0,768},{256,0},{512,256},{768,512},{1,769},{257,1},{513,257},{769... | collective-permute-start | bytes 688136 | tf_op jit(solution)/shard_map/ppermute | solution.py:60
  43.5 9.0 %all-to-all-done = bf16[16,4,512]{2,1,0:T(4,128)(2,1)S(1)} async-done(((bf16[16,4,512]{2,1,0:T(4,128)(2,1)}), bf16[16,4,512]{2,1,0:T(4,128)(2,1)S(1)}, u32[]{:S(2)}, u32[]{:S(2)}) %all-to-all-start) | async-done | bytes 65568 | tf_op jit(solution)/shard_map/all_to_all | solution.py:19
  52.6 0.7 broadcast_in_dim.27
  53.3 6.9 %all-to-all-start.1 = ((bf16[4,64,512]{2,1,0:T(8,128)(2,1)}), bf16[4,64,512]{2,1,0:T(8,128)(2,1)S(1)}, u32[]{:S(2)}, u32[]{:S(2)}) async-start(bf16[4,64,512]{2,1,0:T(8,128)(2,1)} %broadcast_in_dim.27), calls=%async_computation.1 | async-start | bytes 524288 | tf_op jit(solution)/shard_map/all_to_all | solution.py:19
  60.2 1.1 fusion.17
  61.3 4.1 %all-to-all-done.1 = bf16[4,64,512]{2,1,0:T(8,128)(2,1)S(1)} async-done(((bf16[4,64,512]{2,1,0:T(8,128)(2,1)}), bf16[4,64,512]{2,1,0:T(8,128)(2,1)S(1)}, u32[]{:S(2)}, u32[]{:S(2)}) %all-to-all-start.1) | async-done | bytes 262176 | tf_op jit(solution)/shard_map/all_to_all | solution.py:19
  65.4 0.2 convolution_convert_fusion.1
  65.7 0.1 copy.16
  65.8 13.4 %all_to_all.40 = bf16[16,16,224]{2,1,0:T(8,128)(2,1)S(1)} all-to-all(bf16[16,16,224]{2,1,0:T(8,128)(2,1)S(1)} %bitcast.79), channel_id=1, replica_groups=mesh['dp'=4,'zh'=16,'zl'=2,'core'=2,'tensor'=4] {'dp','tensor'}, dimensions={0} | all-to-all | bytes 229376 | tf_op jit(solution)/shard_map/all_to_all | solution.py:19
  79.2 9.9 %all_to_all.41 = bf16[16,16,224]{2,1,0:T(8,128)(2,1)S(1)} all-to-all(bf16[16,16,224]{2,1,0:T(8,128)(2,1)S(1)} %broadcast_in_dim.28), channel_id=1, replica_groups=mesh['dp'=4,'zh'=16,'zl'=2,'core'=2,'tensor'=4] {'dp','tensor'}, dimensions={0} | all-to-all | bytes 229376 | tf_op jit(solution)/shard_map/all_to_all | solution.py:19
  89.1 0.2 convolution_convert_fusion
  89.4 0.1 fusion.18
  89.6 0.1 broadcast_in_dim.29
  89.7 0.1 broadcast_in_dim.30
  89.8 0.1 pad_maximum_fusion.1
  89.9 11.8 %all_to_all.42 = bf16[4,64,640]{2,1,0:T(8,128)(2,1)S(1)} all-to-all(bf16[4,64,640]{2,1,0:T(8,128)(2,1)S(1)} %bitcast.77), channel_id=1, replica_groups=mesh['dp'=4,'zh'=16,'zl'=2,'core'=2,'tensor'=4] {'zl','core'}, dimensions={0} | all-to-all | bytes 655360 | tf_op jit(solution)/shard_map/all_to_all | solution.py:19
  101.7 0.2 add_reduce_fusion.1
  102.1 0.1 pad_maximum_fusion.2
  102.2 38.0 %all_to_all.43 = bf16[16,4,640]{2,1,0:T(4,128)(2,1)S(1)} all-to-all(bf16[16,4,640]{2,1,0:T(4,128)(2,1)S(1)} %reshape.171), channel_id=1, replica_groups=mesh['dp'=4,'zh'=16,'zl'=2,'core'=2,'tensor'=4] {'zh'}, dimensions={0} | all-to-all | bytes 163840 | tf_op jit(solution)/shard_map/all_to_all | solution.py:19
  140.3 0.1 copy.18
  140.5 0.1 copy.19
  140.6 0.1 add_reduce_fusion.2
  141.1 27.9 %all_to_all.44 = bf16[16,4,640]{2,1,0:T(4,128)(2,1)S(1)} all-to-all(bf16[16,4,640]{2,1,0:T(4,128)(2,1)S(1)} %broadcast_in_dim.35), channel_id=1, replica_groups=mesh['dp'=4,'zh'=16,'zl'=2,'core'=2,'tensor'=4] {'zh'}, dimensions={0} | all-to-all | bytes 163840 | tf_op jit(solution)/shard_map/all_to_all | solution.py:19
  169.0 1.2 broadcast_in_dim.37
  170.2 7.9 %all-to-all-start.7 = ((bf16[16,64,640]{2,1,0:T(8,128)(2,1)}), bf16[16,64,640]{2,1,0:T(8,128)(2,1)S(1)}, u32[]{:S(2)}, u32[]{:S(2)}) async-start(bf16[16,64,640]{2,1,0:T(8,128)(2,1)} %broadcast_in_dim.37), calls=%async_computation.7 | async-start | bytes 2621440 | tf_op jit(solution)/shard_map/all_to_all | solution.py:19
  178.1 18.8 %all-to-all-done.7 = bf16[16,64,640]{2,1,0:T(8,128)(2,1)S(1)} async-done(((bf16[16,64,640]{2,1,0:T(8,128)(2,1)}), bf16[16,64,640]{2,1,0:T(8,128)(2,1)S(1)}, u32[]{:S(2)}, u32[]{:S(2)}) %all-to-all-start.7) | async-done | bytes 1310752 | tf_op jit(solution)/shard_map/all_to_all | solution.py:19
  197.0 0.3 fusion
  197.3 6.7 %psum.7 = f32[256]{0:T(256)S(1)} all-reduce(f32[256]{0:T(256)S(1)} %fusion), channel_id=1, replica_groups=mesh['dp'=4,'zh'=16,'zl'=2,'core'=2,'tensor'=4] {'tensor'}, use_global_device_ids=true, to_apply=%region_7.8 | all-reduce | flops 256 | bytes 2048 | tf_op jit(solution)/shard_map/psum | solution.py:101
  204.0 1.4 fusion.1
  205.3 0.2 add_reduce_fusion
  205.6 0.1 fusion.19
  205.7 1.3 fusion.10
  207.0 1.2 fusion.11
  208.2 0.2 fusion.12
  208.5 0.2 fusion.13
  208.7 0.2 fusion.6
  209.0 0.3 fusion.7
  209.2 0.2 fusion.8
  209.5 0.3 fusion.9
  209.8 0.7 convert_divide_fusion.2
  210.5 1.0 pad_maximum_fusion
  211.6 1.0 maximum_bitcast_fusion
  (36 shorter events, 1.2 us)
Async XLA Ops:
  0.6 0.8 copy-start
  2.1 50.5 %all-to-all-start = ((bf16[16,4,512]{2,1,0:T(4,128)(2,1)}), bf16[16,4,512]{2,1,0:T(4,128)(2,1)S(1)}, u32[]{:S(2)}, u32[]{:S(2)}) async-start(bf16[16,4,512]{2,1,0:T(4,128)(2,1)} %broadcast_in_dim.26), calls=%async_computation | async-start | bytes 131072 | tf_op jit(solution)/shard_map/all_to_all | solution.py:19
  31.1 29.1 %copy-start.2 = (bf16[1,224,2048]{2,1,0:T(8,128)(2,1)S(1)}, bf16[1,224,2048]{2,1,0:T(8,128)(2,1)}, u32[]{:S(2)}) copy-start(bf16[1,224,2048]{2,1,0:T(8,128)(2,1)} %param.4) | copy-start | bytes 2752516
  32.8 19.8 %collective-permute-start = (bf16[224,512]{1,0:T(8,128)(2,1)S(1)}, bf16[224,512]{1,0:T(8,128)(2,1)S(1)}, u32[]{:S(2)}, u32[]{:S(2)}) collective-permute-start(bf16[224,512]{1,0:T(8,128)(2,1)S(1)} %get-tuple-element.13), channel_id=1, source_target_pairs={{0,256},{256,512},{512,768},{768,0},{1,257},{257,513},{513,769},{7... | collective-permute-start | bytes 688136 | tf_op jit(solution)/shard_map/ppermute | solution.py:60
  36.0 16.6 %collective-permute-start.1 = (bf16[224,512]{1,0:T(8,128)(2,1)S(1)}, bf16[224,512]{1,0:T(8,128)(2,1)S(1)}, u32[]{:S(2)}, u32[]{:S(2)}) collective-permute-start(bf16[224,512]{1,0:T(8,128)(2,1)S(1)} %get-tuple-element.12), channel_id=1, source_target_pairs={{0,512},{256,768},{512,0},{768,256},{1,513},{257,769},{513,1},{769... | collective-permute-start | bytes 688136 | tf_op jit(solution)/shard_map/ppermute | solution.py:60
  40.5 12.1 %collective-permute-start.2 = (bf16[224,512]{1,0:T(8,128)(2,1)S(1)}, bf16[224,512]{1,0:T(8,128)(2,1)S(1)}, u32[]{:S(2)}, u32[]{:S(2)}) collective-permute-start(bf16[224,512]{1,0:T(8,128)(2,1)S(1)} %get-tuple-element.11), channel_id=1, source_target_pairs={{0,768},{256,0},{512,256},{768,512},{1,769},{257,1},{513,257},{769... | collective-permute-start | bytes 688136 | tf_op jit(solution)/shard_map/ppermute | solution.py:60
  53.3 12.1 %all-to-all-start.1 = ((bf16[4,64,512]{2,1,0:T(8,128)(2,1)}), bf16[4,64,512]{2,1,0:T(8,128)(2,1)S(1)}, u32[]{:S(2)}, u32[]{:S(2)}) async-start(bf16[4,64,512]{2,1,0:T(8,128)(2,1)} %broadcast_in_dim.27), calls=%async_computation.1 | async-start | bytes 524288 | tf_op jit(solution)/shard_map/all_to_all | solution.py:19
  170.2 26.7 %all-to-all-start.7 = ((bf16[16,64,640]{2,1,0:T(8,128)(2,1)}), bf16[16,64,640]{2,1,0:T(8,128)(2,1)S(1)}, u32[]{:S(2)}, u32[]{:S(2)}) async-start(bf16[16,64,640]{2,1,0:T(8,128)(2,1)} %broadcast_in_dim.37), calls=%async_computation.7 | async-start | bytes 2621440 | tf_op jit(solution)/shard_map/all_to_all | solution.py:19
  205.6 2.7 %copy-start.1 = (bf16[4,256,512]{2,1,0:T(8,128)(2,1)S(1)}, bf16[4,256,512]{2,1,0:T(8,128)(2,1)}, u32[]{:S(2)}) copy-start(bf16[4,256,512]{2,1,0:T(8,128)(2,1)} %fusion.1) | copy-start | bytes 3145732
  205.7 3.0 %copy-start.3 = (bf16[1,224,2048]{2,1,0:T(8,128)(2,1)S(1)}, bf16[1,224,2048]{2,1,0:T(8,128)(2,1)}, u32[]{:S(2)}) copy-start(bf16[1,224,2048]{2,1,0:T(8,128)(2,1)} %param.3) | copy-start | bytes 2752516

commit v2 on v1

v2 whole, which is shorter than its diff:
```python
import functools

import jax
import jax.numpy as jnp
from jax import lax
from jax.experimental import pallas as pl
from jax.experimental.pallas import tpu as pltpu
from jax.sharding import Mesh, PartitionSpec as P

D = 8192
FF = 14336
RANK = 256

epsilon = 1e-06
f32 = jnp.float32
bf16 = jnp.bfloat16

NEAR = ("core", "zl")
LANES = 128


def exchange(blocks, axes, first=0):
    groups = None
    if first:
        count = lax.axis_size(axes)
        groups = [[(i + first) % count for i in range(count)]]
    return lax.all_to_all(blocks, axes, 0, 0, axis_index_groups=groups, tiled=False)


def gather(block, axes, first=0):
    count = lax.axis_size(axes)
    return exchange(jnp.broadcast_to(block[None], (count,) + block.shape), axes, first)


def pair_lanes(values):
    high = lax.reduce_precision(values, 8, 7)
    low = (values - high).astype(bf16)
    high = high.astype(bf16)
    rows = values.shape[0]
    half = (rows, LANES // 2)
    return jnp.concatenate(
        [jnp.broadcast_to(high[:, None], half), jnp.broadcast_to(low[:, None], half)], axis=1
    )


def from_lanes(lanes):
    return lanes[..., 0].astype(f32) + lanes[..., LANES // 2].astype(f32)


def finish_kernel(
    scale, core_ref, left_ref, norms_ref, mine_ref, other_ref, m_ref, g_ref, next_ref, update_ref, lefts, rights
):
    rows = left_ref.shape[0]
    pair, block, part = mine_ref.shape
    core = core_ref[0]

    @pl.when(pl.program_id(0) == 0)
    def _():
        hat = left_ref[...].astype(f32) / norms_ref[0:1]
        lefts[:rows] = hat.astype(bf16)
        lefts[rows:] = (hat / norms_ref[1:2]).astype(bf16)

    rights[core] = mine_ref[...].reshape(pair * block, part)
    rights[1 - core] = other_ref[...].reshape(pair * block, part)
    products = jnp.dot(
        lefts[...], rights[...].reshape(2 * pair * block, part), preferred_element_type=f32
    )
    buffer = m_ref[...].astype(f32) + g_ref[...].astype(f32)
    next_ref[...] = (buffer - 0.05 * products[:rows]).astype(bf16)
    update_ref[...] = (products[rows:] * scale).astype(bf16)


def finish(core, left, norms, mine, other, momentum, gradient, scale):
    replicas, pair, block, _ = mine.shape
    rows, rank = left.shape
    part = mine.shape[3] - LANES
    tile = pl.BlockSpec((rows, part), lambda d: (0, d))
    right = pl.BlockSpec((None, pair, block, part), lambda d: (d, 0, 0, 0))
    wide = jax.ShapeDtypeStruct((rows, replicas * part), bf16)
    return pl.pallas_call(
        functools.partial(finish_kernel, scale),
        grid=(replicas,),
        in_specs=[
            pl.BlockSpec(memory_space=pltpu.SMEM),
            pl.BlockSpec((rows, rank), lambda d: (0, 0)),
            pl.BlockSpec((2, rank), lambda d: (0, 0)),
            right,
            right,
            tile,
            tile,
        ],
        out_specs=[tile, tile],
        out_shape=[wide, wide],
        scratch_shapes=[pltpu.VMEM((2 * rows, rank), bf16), pltpu.VMEM((2, rank // 2, part), bf16)],
        compiler_params=pltpu.CompilerParams(vmem_limit_bytes=24 * 1024 * 1024),
    )(core[None], left, norms, mine, other, momentum, gradient)


def body(momentum, gradient, basis):
    replicas = lax.axis_size("dp")
    far = lax.axis_size("zh")
    near = lax.axis_size(NEAR)
    me = lax.axis_index("dp")
    core = lax.axis_index("core")
    own_rows, width = basis.shape
    part = width // replicas
    rank = own_rows * far * near
    half = rank // 2

    own_basis = lax.dynamic_slice_in_dim(basis, me * part, part, 1).astype(bf16)
    far_basis = gather(own_basis, "zh", far // 2).reshape(far * own_rows, part)

    def column_block(index):
        first = lax.dynamic_slice_in_dim(momentum[0], index * part, part, 1).astype(f32)
        second = lax.dynamic_slice_in_dim(gradient[0], index * part, part, 1).astype(f32)
        return (first + second).astype(bf16)

    pieces = [
        lax.ppermute(
            column_block((me + k) % replicas), "dp", [(i, (i + k) % replicas) for i in range(replicas)]
        )
        for k in range(1, replicas)
    ]
    far_basis, *pieces = lax.optimization_barrier((far_basis, *pieces))
    basis_h = gather(far_basis, NEAR).reshape(rank, part)
    total = column_block(me).astype(f32)
    for piece in pieces:
        total = total + piece.astype(f32)
    mean_h = (total / replicas).astype(bf16)

    left = lax.dot_general(basis_h, mean_h, (((1,), (1,)), ((), ())), preferred_element_type=f32).T
    left = jnp.sum(gather(left.astype(bf16), "tensor").astype(f32), axis=0)
    left = jnp.sum(gather(left.astype(bf16), "dp").astype(f32), axis=0)
    squares = jnp.sum(left * left, axis=0)
    left_h = left.astype(bf16)

    right_term = lax.dot_general(
        left_h, mean_h, (((0,), (0,)), ((), ())), preferred_element_type=f32
    ).astype(bf16)
    packed = jnp.concatenate([right_term, pair_lanes(squares)], axis=1)
    packed = exchange(packed.reshape(near, rank // near, part + LANES), NEAR)
    right_near = jnp.sum(packed[..., :part].astype(f32), axis=0)
    squares_near = jnp.sum(from_lanes(packed[..., part:]), axis=0)
    packed = jnp.concatenate([right_near.astype(bf16), pair_lanes(squares_near)], axis=1)
    packed = exchange(packed.reshape(far, own_rows, part + LANES), "zh")
    right_un = jnp.sum(packed[..., :part].astype(f32), axis=0)
    norms = jnp.sqrt(jnp.sum(from_lanes(packed[..., part:]), axis=0) + epsilon)
    right_own = (right_un / norms[:, None]).astype(bf16)

    packed = jnp.concatenate([right_own, pair_lanes(norms)], axis=1)
    packed = gather(packed, "zh").reshape(far * own_rows, part + LANES)
    packed = gather(packed, ("dp", "zl")).reshape(replicas, 2, half // 2, part + LANES)
    other = lax.ppermute(packed, "core", [(0, 1), (1, 0)])

    right_wide = packed[..., :part].astype(f32)
    right_squares = jnp.sum(right_wide * right_wide, axis=(0, 3)).reshape(1, half)
    left_norms = from_lanes(packed[0, ..., part:]).reshape(1, half)
    both = gather(jnp.concatenate([left_norms, right_squares]), ("core", "tensor"))
    both = both.reshape(2, -1, 2, half)
    right_norms = jnp.sqrt(jnp.sum(both[:, :, 1], axis=1) + epsilon).reshape(rank)
    norms = jnp.stack([both[:, 0, 0].reshape(rank), right_norms])
    momentum_next, update = finish(
        core, left_h, norms, packed, other, momentum[0], gradient[0], (FF * D / RANK) ** 0.5
    )

    place = (lax.axis_index("zh") + far // 2) % far
    pair = lax.axis_index("zl")
    rows = lax.dynamic_slice(
        packed, (0, pair, place * own_rows, 0), (replicas, 1, own_rows, part)
    )[:, 0]
    first = core * half + pair * (half // 2) + place * own_rows
    own_norms = lax.dynamic_slice(right_norms, (first,), (own_rows,))
    basis_next = (
        (rows.astype(f32) / own_norms[None, :, None]).transpose(1, 0, 2).reshape(own_rows, width)
    )
    return (momentum_next[None], update, basis_next)


def solution(mesh):
    replicas, fsdp, tensor = (mesh.shape[name] for name in ("dp", "fsdp", "tensor"))
    fine = Mesh(
        mesh.devices.reshape(replicas, fsdp // 4, 2, 2, tensor), ("dp", "zh", "zl", "core", "tensor")
    )
    z = ("zh", "zl", "core")
    return jax.shard_map(
        body,
        mesh=fine,
        in_specs=(P("dp", z, "tensor"), P("dp", z, "tensor"), P(z, "tensor")),
        out_specs=(P("dp", z, "tensor"), P(z, "tensor"), P(z, "tensor")),
        check_vma=False,
    )
```

time: 214 us -> 190 us (0.89)
  waiting for transfers between devices: 31.9 us -> 13.9 us
  starting transfers between devices: 54.5 us -> 62.3 us
  blocking collectives: 108 us -> 101 us
  other arithmetic: 8.37 us -> 3.87 us
  matrix products: 4.42 us -> 0.5 us
  Pallas kernels: 0 us -> 2.58 us
    all_to_all x3, waiting for transfers between devices: 31.9 us -> 7.83 us  [exchange(): lax.all_to_all(blocks, axes, 0, 0, axis_index_groups=groups, tiled=False)]
    psum x1 -> x0, blocking collectives: 6.65 us -> none  [body(): lax.psum(jnp.sum(right_wide * right_wide, axis=(0, 2)), 'tensor')]
    ppermute x3, waiting for transfers between devices: 0.01 us -> 6.05 us  [body(): lax.ppermute(column_block((me + k) % replicas), 'dp', [(i, (i + k) % repl...]
    all_to_all x3, starting transfers between devices: 43.8 us -> 49.4 us  [exchange(): lax.all_to_all(blocks, axes, 0, 0, axis_index_groups=groups, tiled=False)]
    dot_general x9 -> x1, matrix products: 4.18 us -> 0.24 us  [body(): lax.dot_general(left_h, mean_h, (((0,), (0,)), ((), ())), preferred_eleme...]
    pallas_call x0 -> x1, Pallas kernels: none -> 2.58 us  [finish(): pl.pallas_call(functools.partial(finish_kernel, scale), grid=(replicas,),...]
    all_to_all x5 -> x6, blocking collectives: 101 us -> 101 us  [exchange(): lax.all_to_all(blocks, axes, 0, 0, axis_index_groups=groups, tiled=False)]
  transfers between devices with their start and end apart: 6 -> 7, of which waited for: 3 -> 4; matrix products, arithmetic and copies ran while one was open for 1% -> 1% of each run, Pallas kernels for 0% -> 0%
where the time goes in v2:
time: 190 us; the launch traced here: 189 us
  blocking collectives  101 us (53%)
  starting transfers between devices  62.3 us (33%)
  waiting for transfers between devices  13.9 us (7%)
  local copies, waits for them, and re-layouts  4.04 us (2%)
  other arithmetic  3.87 us (2%)
  Pallas kernels  2.58 us (1%)
    all_to_all x6, blocking collectives, exchange(): lax.all_to_all(blocks, axes, 0, 0, axis_index_groups=groups, tiled=False)  101 us
    all_to_all x3, starting transfers between devices, exchange(): lax.all_to_all(blocks, axes, 0, 0, axis_index_groups=groups, tiled=False)  49.4 us
    ppermute x3, starting transfers between devices, body(): lax.ppermute(column_block((me + k) % replicas), 'dp', [(i, (i + k) % repl...  10.8 us
    all_to_all x3, waiting for transfers between devices, exchange(): lax.all_to_all(blocks, axes, 0, 0, axis_index_groups=groups, tiled=False)  7.83 us
    ppermute x3, waiting for transfers between devices, body(): lax.ppermute(column_block((me + k) % replicas), 'dp', [(i, (i + k) % repl...  6.05 us
  transfers between devices with their start and end apart: 7, of which 4 were waited for; matrix products, arithmetic and copies ran while one was open for 1% of the time, Pallas kernels for 0%

profile of v2, /device:TPU:1, one launch (start us, length us, event | category | flops | bytes accessed | tf_op | source)
XLA Modules:
  0.0 189.0 jit_solution(14644088618092950850)
XLA Ops:
  0.7 0.7 copy-done
  1.4 0.7 broadcast_in_dim.33
  2.1 35.6 %all-to-all-start = ((bf16[16,4,512]{2,1,0:T(4,128)(2,1)}), bf16[16,4,512]{2,1,0:T(4,128)(2,1)S(1)}, u32[]{:S(2)}, u32[]{:S(2)}) async-start(bf16[16,4,512]{2,1,0:T(4,128)(2,1)} %broadcast_in_dim.33), calls=%async_computation | async-start | bytes 131072 | tf_op jit(solution)/shard_map/all_to_all | solution.py:27
  37.6 1.7 fusion.7
  39.3 3.3 %collective-permute-start = (bf16[224,512]{1,0:T(8,128)(2,1)S(1)}, bf16[224,512]{1,0:T(8,128)(2,1)S(1)}, u32[]{:S(2)}, u32[]{:S(2)}) collective-permute-start(bf16[224,512]{1,0:T(8,128)(2,1)S(1)} %get-tuple-element.17), channel_id=1, source_target_pairs={{0,256},{256,512},{512,768},{768,0},{1,257},{257,513},{513,769},{7... | collective-permute-start | bytes 688136 | tf_op jit(solution)/shard_map/ppermute | solution.py:119
  42.7 4.5 %collective-permute-start.1 = (bf16[224,512]{1,0:T(8,128)(2,1)S(1)}, bf16[224,512]{1,0:T(8,128)(2,1)S(1)}, u32[]{:S(2)}, u32[]{:S(2)}) collective-permute-start(bf16[224,512]{1,0:T(8,128)(2,1)S(1)} %get-tuple-element.16), channel_id=1, source_target_pairs={{0,512},{256,768},{512,0},{768,256},{1,513},{257,769},{513,1},{769... | collective-permute-start | bytes 688136 | tf_op jit(solution)/shard_map/ppermute | solution.py:119
  47.2 3.0 %collective-permute-start.2 = (bf16[224,512]{1,0:T(8,128)(2,1)S(1)}, bf16[224,512]{1,0:T(8,128)(2,1)S(1)}, u32[]{:S(2)}, u32[]{:S(2)}) collective-permute-start(bf16[224,512]{1,0:T(8,128)(2,1)S(1)} %get-tuple-element.15), channel_id=1, source_target_pairs={{0,768},{256,0},{512,256},{768,512},{1,769},{257,1},{513,257},{769... | collective-permute-start | bytes 688136 | tf_op jit(solution)/shard_map/ppermute | solution.py:119
  50.2 4.3 %collective-permute-done.1 = bf16[224,512]{1,0:T(8,128)(2,1)S(1)} collective-permute-done((bf16[224,512]{1,0:T(8,128)(2,1)S(1)}, bf16[224,512]{1,0:T(8,128)(2,1)S(1)}, u32[]{:S(2)}, u32[]{:S(2)}) %collective-permute-start.1) | collective-permute-done | bytes 229408 | tf_op jit(solution)/shard_map/ppermute | solution.py:119
  54.6 1.7 collective-permute-done.2
  56.3 0.7 broadcast_in_dim.34
  57.0 5.2 %all-to-all-start.1 = ((bf16[4,64,512]{2,1,0:T(8,128)(2,1)}), bf16[4,64,512]{2,1,0:T(8,128)(2,1)S(1)}, u32[]{:S(2)}, u32[]{:S(2)}) async-start(bf16[4,64,512]{2,1,0:T(8,128)(2,1)} %broadcast_in_dim.34), calls=%async_computation.1 | async-start | bytes 524288 | tf_op jit(solution)/shard_map/all_to_all | solution.py:27
  62.2 0.2 fusion.3
  62.3 5.0 %all-to-all-done.1 = bf16[4,64,512]{2,1,0:T(8,128)(2,1)S(1)} async-done(((bf16[4,64,512]{2,1,0:T(8,128)(2,1)}), bf16[4,64,512]{2,1,0:T(8,128)(2,1)S(1)}, u32[]{:S(2)}, u32[]{:S(2)}) %all-to-all-start.1) | async-done | bytes 262176 | tf_op jit(solution)/shard_map/all_to_all | solution.py:27
  67.3 0.3 convolution_convert_fusion.1
  67.6 11.3 %all_to_all.45 = bf16[4,224,256]{2,1,0:T(8,128)(2,1)S(1)} all-to-all(bf16[4,224,256]{2,1,0:T(8,128)(2,1)S(1)} %broadcast_in_dim.35), channel_id=1, replica_groups=mesh['dp'=4,'zh'=16,'zl'=2,'core'=2,'tensor'=4] {'tensor'}, dimensions={0} | all-to-all | bytes 917504 | tf_op jit(solution)/shard_map/all_to_all | solution.py:27
  78.9 0.1 reduce_sum.87
  79.0 10.5 %all_to_all.46 = bf16[4,224,256]{2,1,0:T(8,128)(2,1)S(1)} all-to-all(bf16[4,224,256]{2,1,0:T(8,128)(2,1)S(1)} %broadcast_in_dim.36), channel_id=1, replica_groups=mesh['dp'=4,'zh'=16,'zl'=2,'core'=2,'tensor'=4] {'dp'}, dimensions={0} | all-to-all | bytes 917504 | tf_op jit(solution)/shard_map/all_to_all | solution.py:27
  89.7 0.2 convolution_convert_fusion
  89.9 0.1 broadcast_in_dim.38
  90.0 0.1 broadcast_in_dim.37
  90.1 0.1 pad_maximum_fusion
  90.2 12.0 %all_to_all.47 = bf16[4,64,640]{2,1,0:T(8,128)(2,1)S(1)} all-to-all(bf16[4,64,640]{2,1,0:T(8,128)(2,1)S(1)} %bitcast.43), channel_id=1, replica_groups=mesh['dp'=4,'zh'=16,'zl'=2,'core'=2,'tensor'=4] {'core','zl'}, dimensions={0} | all-to-all | bytes 655360 | tf_op jit(solution)/shard_map/all_to_all | solution.py:27
  102.3 0.2 add_reduce_fusion
  102.5 0.1 broadcast_in_dim.40
  102.6 0.1 broadcast_in_dim.39
  102.7 0.1 pad_maximum_fusion.1
  102.8 27.7 %all_to_all.48 = bf16[16,4,640]{2,1,0:T(4,128)(2,1)S(1)} all-to-all(bf16[16,4,640]{2,1,0:T(4,128)(2,1)S(1)} %reshape.151), channel_id=1, replica_groups=mesh['dp'=4,'zh'=16,'zl'=2,'core'=2,'tensor'=4] {'zh'}, dimensions={0} | all-to-all | bytes 163840 | tf_op jit(solution)/shard_map/all_to_all | solution.py:27
  130.5 0.1 fusion.12
  130.6 0.1 copy.18
  130.7 0.1 copy.17
  130.8 0.1 add_reduce_fusion.2
  131.0 0.1 divide_convert_fusion
  131.1 0.1 broadcast_in_dim.42
  131.2 0.1 broadcast_in_dim.41
  131.3 0.1 pad_maximum_fusion.2
  131.4 28.7 %all_to_all.49 = bf16[16,4,640]{2,1,0:T(4,128)(2,1)S(1)} all-to-all(bf16[16,4,640]{2,1,0:T(4,128)(2,1)S(1)} %broadcast_in_dim.43), channel_id=1, replica_groups=mesh['dp'=4,'zh'=16,'zl'=2,'core'=2,'tensor'=4] {'zh'}, dimensions={0} | all-to-all | bytes 163840 | tf_op jit(solution)/shard_map/all_to_all | solution.py:27
  160.1 10.8 %all_to_all.50 = bf16[8,64,640]{2,1,0:T(8,128)(2,1)S(1)} all-to-all(bf16[8,64,640]{2,1,0:T(8,128)(2,1)S(1)} %broadcast_in_dim.45), channel_id=1, replica_groups=mesh['dp'=4,'zh'=16,'zl'=2,'core'=2,'tensor'=4] {'dp','zl'}, dimensions={0} | all-to-all | bytes 1310720 | tf_op jit(solution)/shard_map/all_to_all | solution.py:27
  170.9 0.2 multiply_reduce_fusion
  171.1 0.1 reshape.153
  171.2 0.2 add_reduce_fusion.1
  171.3 0.1 add.153
  171.4 0.6 broadcast_in_dim.46
  172.0 8.7 %all-to-all-start.8 = ((f32[8,2,128]{2,1,0:T(2,128)}), f32[8,2,128]{2,1,0:T(2,128)S(1)}, u32[]{:S(2)}, u32[]{:S(2)}) async-start(f32[8,2,128]{2,1,0:T(2,128)} %broadcast_in_dim.46), calls=%async_computation.8 | async-start | bytes 16384 | tf_op jit(solution)/shard_map/all_to_all | solution.py:27
  180.7 2.0 %collective-permute-start.3 = (bf16[4,2,64,640]{3,2,1,0:T(8,128)(2,1)S(1)}, bf16[4,2,64,640]{3,2,1,0:T(8,128)(2,1)S(1)}, u32[]{:S(2)}, u32[]{:S(2)}) collective-permute-start(bf16[4,2,64,640]{3,2,1,0:T(8,128)(2,1)S(1)} %bitcast.38), channel_id=1, source_target_pairs={{0,4},{4,0},{1,5},{5,1},{2,6},{6,2},{3,7},{7,3},{8,12},{12,8},{9,1... | collective-permute-start | bytes 1966088 | tf_op jit(solution)/shard_map/ppermute | solution.py:153
  182.8 2.8 %all-to-all-done.8 = f32[8,2,128]{2,1,0:T(2,128)S(1)} async-done(((f32[8,2,128]{2,1,0:T(2,128)}), f32[8,2,128]{2,1,0:T(2,128)S(1)}, u32[]{:S(2)}, u32[]{:S(2)}) %all-to-all-start.8) | async-done | bytes 8224 | tf_op jit(solution)/shard_map/all_to_all | solution.py:27
  185.7 0.1 dynamic_slice.43
  185.7 0.7 convert_divide_fusion
  186.5 2.6 %shard_map.58 = (bf16[224,2048]{1,0:T(8,128)(2,1)}, bf16[224,2048]{1,0:T(8,128)(2,1)}) custom-call(s32[1]{0:T(128)} %bitcast.core_ref, bf16[224,256]{1,0:T(8,128)(2,1)S(1)} %get-tuple-element.19.left_ref, f32[2,256]{1,0:T(2,128)S(1)} %pad_maximum_fusion.3.norms_ref, bf16[4,2,64,640]{3,2,1,0:T(8,128)(2,1)S(1)} %bitcast.40, ...), custom_call_target="tpu_custom_call" | custom-call | tf_op jit(solution)/shard_map/pallas_call | solution.py:80
  (31 shorter events, 0.5 us)
Async XLA Ops:
  0.6 0.8 copy-start
  2.1 48.1 %all-to-all-start = ((bf16[16,4,512]{2,1,0:T(4,128)(2,1)}), bf16[16,4,512]{2,1,0:T(4,128)(2,1)S(1)}, u32[]{:S(2)}, u32[]{:S(2)}) async-start(bf16[16,4,512]{2,1,0:T(4,128)(2,1)} %broadcast_in_dim.33), calls=%async_computation | async-start | bytes 131072 | tf_op jit(solution)/shard_map/all_to_all | solution.py:27
  37.6 24.5 %copy-start.2 = (bf16[1,224,2048]{2,1,0:T(8,128)(2,1)S(1)}, bf16[1,224,2048]{2,1,0:T(8,128)(2,1)}, u32[]{:S(2)}) copy-start(bf16[1,224,2048]{2,1,0:T(8,128)(2,1)} %param.3) | copy-start | bytes 2752516
  39.3 22.9 %copy-start.1 = (bf16[1,224,2048]{2,1,0:T(8,128)(2,1)S(1)}, bf16[1,224,2048]{2,1,0:T(8,128)(2,1)}, u32[]{:S(2)}) copy-start(bf16[1,224,2048]{2,1,0:T(8,128)(2,1)} %param.4) | copy-start | bytes 2752516
  39.3 10.9 %collective-permute-start = (bf16[224,512]{1,0:T(8,128)(2,1)S(1)}, bf16[224,512]{1,0:T(8,128)(2,1)S(1)}, u32[]{:S(2)}, u32[]{:S(2)}) collective-permute-start(bf16[224,512]{1,0:T(8,128)(2,1)S(1)} %get-tuple-element.17), channel_id=1, source_target_pairs={{0,256},{256,512},{512,768},{768,0},{1,257},{257,513},{513,769},{7... | collective-permute-start | bytes 688136 | tf_op jit(solution)/shard_map/ppermute | solution.py:119
  42.7 11.9 %collective-permute-start.1 = (bf16[224,512]{1,0:T(8,128)(2,1)S(1)}, bf16[224,512]{1,0:T(8,128)(2,1)S(1)}, u32[]{:S(2)}, u32[]{:S(2)}) collective-permute-start(bf16[224,512]{1,0:T(8,128)(2,1)S(1)} %get-tuple-element.16), channel_id=1, source_target_pairs={{0,512},{256,768},{512,0},{768,256},{1,513},{257,769},{513,1},{769... | collective-permute-start | bytes 688136 | tf_op jit(solution)/shard_map/ppermute | solution.py:119
  47.2 9.1 %collective-permute-start.2 = (bf16[224,512]{1,0:T(8,128)(2,1)S(1)}, bf16[224,512]{1,0:T(8,128)(2,1)S(1)}, u32[]{:S(2)}, u32[]{:S(2)}) collective-permute-start(bf16[224,512]{1,0:T(8,128)(2,1)S(1)} %get-tuple-element.15), channel_id=1, source_target_pairs={{0,768},{256,0},{512,256},{768,512},{1,769},{257,1},{513,257},{769... | collective-permute-start | bytes 688136 | tf_op jit(solution)/shard_map/ppermute | solution.py:119
  57.0 10.3 %all-to-all-start.1 = ((bf16[4,64,512]{2,1,0:T(8,128)(2,1)}), bf16[4,64,512]{2,1,0:T(8,128)(2,1)S(1)}, u32[]{:S(2)}, u32[]{:S(2)}) async-start(bf16[4,64,512]{2,1,0:T(8,128)(2,1)} %broadcast_in_dim.34), calls=%async_computation.1 | async-start | bytes 524288 | tf_op jit(solution)/shard_map/all_to_all | solution.py:27
  172.0 13.6 %all-to-all-start.8 = ((f32[8,2,128]{2,1,0:T(2,128)}), f32[8,2,128]{2,1,0:T(2,128)S(1)}, u32[]{:S(2)}, u32[]{:S(2)}) async-start(f32[8,2,128]{2,1,0:T(2,128)} %broadcast_in_dim.46), calls=%async_computation.8 | async-start | bytes 16384 | tf_op jit(solution)/shard_map/all_to_all | solution.py:27
  180.7 5.7 %collective-permute-start.3 = (bf16[4,2,64,640]{3,2,1,0:T(8,128)(2,1)S(1)}, bf16[4,2,64,640]{3,2,1,0:T(8,128)(2,1)S(1)}, u32[]{:S(2)}, u32[]{:S(2)}) collective-permute-start(bf16[4,2,64,640]{3,2,1,0:T(8,128)(2,1)S(1)} %bitcast.38), channel_id=1, source_target_pairs={{0,4},{4,0},{1,5},{5,1},{2,6},{6,2},{3,7},{7,3},{8,12},{12,8},{9,1... | collective-permute-start | bytes 1966088 | tf_op jit(solution)/shard_map/ppermute | solution.py:153

commit v3 on v2

--- a/solution.py
+++ b/solution.py
@@ -48,7 +48,8 @@
 
 
 def finish_kernel(
-    scale, core_ref, left_ref, norms_ref, mine_ref, other_ref, m_ref, g_ref, next_ref, update_ref, lefts, rights
+    scale, core_ref, left_ref, norms_ref, mine_ref, other_ref, m_ref, g_ref, own_ref, own_norms_ref,
+    next_ref, update_ref, basis_ref, lefts, rights
 ):
     rows = left_ref.shape[0]
     pair, block, part = mine_ref.shape
@@ -68,9 +69,10 @@
     buffer = m_ref[...].astype(f32) + g_ref[...].astype(f32)
     next_ref[...] = (buffer - 0.05 * products[:rows]).astype(bf16)
     update_ref[...] = (products[rows:] * scale).astype(bf16)
+    basis_ref[...] = own_ref[...].astype(f32) / own_norms_ref[...]
 
 
-def finish(core, left, norms, mine, other, momentum, gradient, scale):
+def finish(core, left, norms, mine, other, momentum, gradient, own, own_norms, scale):
     replicas, pair, block, _ = mine.shape
     rows, rank = left.shape
     part = mine.shape[3] - LANES
@@ -88,12 +90,14 @@
             right,
             tile,
             tile,
+            pl.BlockSpec((None, own.shape[1], part), lambda d: (d, 0, 0)),
+            pl.BlockSpec(own_norms.shape, lambda d: (0, 0)),
         ],
-        out_specs=[tile, tile],
-        out_shape=[wide, wide],
+        out_specs=[tile, tile, pl.BlockSpec((own.shape[1], part), lambda d: (0, d))],
+        out_shape=[wide, wide, jax.ShapeDtypeStruct((own.shape[1], replicas * part), f32)],
         scratch_shapes=[pltpu.VMEM((2 * rows, rank), bf16), pltpu.VMEM((2, rank // 2, part), bf16)],
         compiler_params=pltpu.CompilerParams(vmem_limit_bytes=24 * 1024 * 1024),
-    )(core[None], left, norms, mine, other, momentum, gradient)
+    )(core[None], left, norms, mine, other, momentum, gradient, own, own_norms)
 
 
 def body(momentum, gradient, basis):
@@ -121,12 +125,12 @@
         )
         for k in range(1, replicas)
     ]
-    far_basis, *pieces = lax.optimization_barrier((far_basis, *pieces))
-    basis_h = gather(far_basis, NEAR).reshape(rank, part)
     total = column_block(me).astype(f32)
     for piece in pieces:
         total = total + piece.astype(f32)
     mean_h = (total / replicas).astype(bf16)
+    far_basis, mean_h = lax.optimization_barrier((far_basis, mean_h))
+    basis_h = gather(far_basis, NEAR).reshape(rank, part)
 
     left = lax.dot_general(basis_h, mean_h, (((1,), (1,)), ((), ())), preferred_element_type=f32).T
     left = jnp.sum(gather(left.astype(bf16), "tensor").astype(f32), axis=0)
@@ -142,13 +146,13 @@
     right_near = jnp.sum(packed[..., :part].astype(f32), axis=0)
     squares_near = jnp.sum(from_lanes(packed[..., part:]), axis=0)
     packed = jnp.concatenate([right_near.astype(bf16), pair_lanes(squares_near)], axis=1)
-    packed = exchange(packed.reshape(far, own_rows, part + LANES), "zh")
+    packed = exchange(packed.reshape(far, own_rows, part + LANES), "zh", far // 8)
     right_un = jnp.sum(packed[..., :part].astype(f32), axis=0)
     norms = jnp.sqrt(jnp.sum(from_lanes(packed[..., part:]), axis=0) + epsilon)
     right_own = (right_un / norms[:, None]).astype(bf16)
 
     packed = jnp.concatenate([right_own, pair_lanes(norms)], axis=1)
-    packed = gather(packed, "zh").reshape(far * own_rows, part + LANES)
+    packed = gather(packed, "zh", far // 8).reshape(far * own_rows, part + LANES)
     packed = gather(packed, ("dp", "zl")).reshape(replicas, 2, half // 2, part + LANES)
     other = lax.ppermute(packed, "core", [(0, 1), (1, 0)])
 
@@ -159,19 +163,17 @@
     both = both.reshape(2, -1, 2, half)
     right_norms = jnp.sqrt(jnp.sum(both[:, :, 1], axis=1) + epsilon).reshape(rank)
     norms = jnp.stack([both[:, 0, 0].reshape(rank), right_norms])
-    momentum_next, update = finish(
-        core, left_h, norms, packed, other, momentum[0], gradient[0], (FF * D / RANK) ** 0.5
-    )
-
     place = (lax.axis_index("zh") + far // 2) % far
     pair = lax.axis_index("zl")
-    rows = lax.dynamic_slice(
-        packed, (0, pair, place * own_rows, 0), (replicas, 1, own_rows, part)
+    gathered, right_norms = lax.optimization_barrier((packed, right_norms))
+    own = lax.dynamic_slice(
+        gathered, (0, pair, place * own_rows, 0), (replicas, 1, own_rows, part)
     )[:, 0]
     first = core * half + pair * (half // 2) + place * own_rows
-    own_norms = lax.dynamic_slice(right_norms, (first,), (own_rows,))
-    basis_next = (
-        (rows.astype(f32) / own_norms[None, :, None]).transpose(1, 0, 2).reshape(own_rows, width)
+    own_norms = lax.dynamic_slice(right_norms, (first,), (own_rows,))[:, None]
+    momentum_next, update, basis_next = finish(
+        core, left_h, norms, packed, other, momentum[0], gradient[0], own, own_norms,
+        (FF * D / RANK) ** 0.5,
     )
     return (momentum_next[None], update, basis_next)
 

time: 190 us -> 186 us (0.979)
  blocking collectives: 101 us -> 109 us
  starting transfers between devices: 62.3 us -> 55.9 us
  waiting for transfers between devices: 13.9 us -> 8.93 us
    all_to_all x6 -> x7, blocking collectives: 101 us -> 109 us  [exchange(): lax.all_to_all(blocks, axes, 0, 0, axis_index_groups=groups, tiled=False)]
    all_to_all x3 -> x2, starting transfers between devices: 49.4 us -> 43.2 us  [exchange(): lax.all_to_all(blocks, axes, 0, 0, axis_index_groups=groups, tiled=False)]
    all_to_all x3 -> x2, waiting for transfers between devices: 7.83 us -> 2.84 us  [exchange(): lax.all_to_all(blocks, axes, 0, 0, axis_index_groups=groups, tiled=False)]
  transfers between devices with their start and end apart: 7 -> 6, of which waited for: 4 -> 3; matrix products, arithmetic and copies ran while one was open for 1% -> 1% of each run, Pallas kernels for 0% -> 0%
where the time goes in v3:
time: 186 us; the launch traced here: 185 us
  blocking collectives  109 us (59%)
  starting transfers between devices  55.9 us (30%)
  waiting for transfers between devices  8.93 us (5%)
  local copies, waits for them, and re-layouts  3.46 us (2%)
  other arithmetic  3.22 us (2%)
  Pallas kernels  2.63 us (1%)
    all_to_all x7, blocking collectives, exchange(): lax.all_to_all(blocks, axes, 0, 0, axis_index_groups=groups, tiled=False)  109 us
    all_to_all x2, starting transfers between devices, exchange(): lax.all_to_all(blocks, axes, 0, 0, axis_index_groups=groups, tiled=False)  43.2 us
    ppermute x3, starting transfers between devices, body(): lax.ppermute(column_block((me + k) % replicas), 'dp', [(i, (i + k) % repl...  10.7 us
    ppermute x3, waiting for transfers between devices, body(): lax.ppermute(column_block((me + k) % replicas), 'dp', [(i, (i + k) % repl...  6.08 us
  transfers between devices with their start and end apart: 6, of which 3 were waited for; matrix products, arithmetic and copies ran while one was open for 1% of the time, Pallas kernels for 0%

profile of v3, /device:TPU:1, one launch (start us, length us, event | category | flops | bytes accessed | tf_op | source)
XLA Modules:
  0.0 184.9 jit_solution(13335345203555184486)
XLA Ops:
  0.7 0.7 copy-done
  1.4 0.7 broadcast_in_dim.35
  2.1 35.6 %all-to-all-start = ((bf16[16,4,512]{2,1,0:T(4,128)(2,1)}), bf16[16,4,512]{2,1,0:T(4,128)(2,1)S(1)}, u32[]{:S(2)}, u32[]{:S(2)}) async-start(bf16[16,4,512]{2,1,0:T(4,128)(2,1)} %broadcast_in_dim.35), calls=%async_computation | async-start | bytes 131072 | tf_op jit(solution)/shard_map/all_to_all | solution.py:27
  37.6 1.7 fusion.5
  39.4 3.2 %collective-permute-start = (bf16[224,512]{1,0:T(8,128)(2,1)S(1)}, bf16[224,512]{1,0:T(8,128)(2,1)S(1)}, u32[]{:S(2)}, u32[]{:S(2)}) collective-permute-start(bf16[224,512]{1,0:T(8,128)(2,1)S(1)} %get-tuple-element.17), channel_id=1, source_target_pairs={{0,256},{256,512},{512,768},{768,0},{1,257},{257,513},{513,769},{7... | collective-permute-start | bytes 688136 | tf_op jit(solution)/shard_map/ppermute | solution.py:123
  42.6 4.5 %collective-permute-start.1 = (bf16[224,512]{1,0:T(8,128)(2,1)S(1)}, bf16[224,512]{1,0:T(8,128)(2,1)S(1)}, u32[]{:S(2)}, u32[]{:S(2)}) collective-permute-start(bf16[224,512]{1,0:T(8,128)(2,1)S(1)} %get-tuple-element.18), channel_id=1, source_target_pairs={{0,512},{256,768},{512,0},{768,256},{1,513},{257,769},{513,1},{769... | collective-permute-start | bytes 688136 | tf_op jit(solution)/shard_map/ppermute | solution.py:123
  47.1 3.0 %collective-permute-start.2 = (bf16[224,512]{1,0:T(8,128)(2,1)S(1)}, bf16[224,512]{1,0:T(8,128)(2,1)S(1)}, u32[]{:S(2)}, u32[]{:S(2)}) collective-permute-start(bf16[224,512]{1,0:T(8,128)(2,1)S(1)} %get-tuple-element.19), channel_id=1, source_target_pairs={{0,768},{256,0},{512,256},{768,512},{1,769},{257,1},{513,257},{769... | collective-permute-start | bytes 688136 | tf_op jit(solution)/shard_map/ppermute | solution.py:123
  50.1 4.4 %collective-permute-done.1 = bf16[224,512]{1,0:T(8,128)(2,1)S(1)} collective-permute-done((bf16[224,512]{1,0:T(8,128)(2,1)S(1)}, bf16[224,512]{1,0:T(8,128)(2,1)S(1)}, u32[]{:S(2)}, u32[]{:S(2)}) %collective-permute-start.1) | collective-permute-done | bytes 229408 | tf_op jit(solution)/shard_map/ppermute | solution.py:123
  54.5 1.7 collective-permute-done.2
  56.2 0.2 fusion.3
  56.4 9.2 %all_to_all.45 = bf16[4,64,512]{2,1,0:T(8,128)(2,1)S(1)} all-to-all(bf16[4,64,512]{2,1,0:T(8,128)(2,1)S(1)} %broadcast_in_dim.36), channel_id=1, replica_groups=mesh['dp'=4,'zh'=16,'zl'=2,'core'=2,'tensor'=4] {'core','zl'}, dimensions={0} | all-to-all | bytes 524288 | tf_op jit(solution)/shard_map/all_to_all | solution.py:27
  65.6 0.2 convolution_convert_fusion.1
  65.9 11.3 %all_to_all.46 = bf16[4,224,256]{2,1,0:T(8,128)(2,1)S(1)} all-to-all(bf16[4,224,256]{2,1,0:T(8,128)(2,1)S(1)} %broadcast_in_dim.37), channel_id=1, replica_groups=mesh['dp'=4,'zh'=16,'zl'=2,'core'=2,'tensor'=4] {'tensor'}, dimensions={0} | all-to-all | bytes 917504 | tf_op jit(solution)/shard_map/all_to_all | solution.py:27
  77.2 0.1 reduce_sum.87
  77.3 10.5 %all_to_all.47 = bf16[4,224,256]{2,1,0:T(8,128)(2,1)S(1)} all-to-all(bf16[4,224,256]{2,1,0:T(8,128)(2,1)S(1)} %broadcast_in_dim.38), channel_id=1, replica_groups=mesh['dp'=4,'zh'=16,'zl'=2,'core'=2,'tensor'=4] {'dp'}, dimensions={0} | all-to-all | bytes 917504 | tf_op jit(solution)/shard_map/all_to_all | solution.py:27
  87.8 0.1 convert_reduce_fusion
  88.0 0.2 convolution_convert_fusion
  88.2 0.1 broadcast_in_dim.39
  88.3 0.1 broadcast_in_dim.40
  88.4 0.1 pad_maximum_fusion
  88.5 12.0 %all_to_all.48 = bf16[4,64,640]{2,1,0:T(8,128)(2,1)S(1)} all-to-all(bf16[4,64,640]{2,1,0:T(8,128)(2,1)S(1)} %bitcast.41), channel_id=1, replica_groups=mesh['dp'=4,'zh'=16,'zl'=2,'core'=2,'tensor'=4] {'core','zl'}, dimensions={0} | all-to-all | bytes 655360 | tf_op jit(solution)/shard_map/all_to_all | solution.py:27
  100.6 0.2 add_reduce_fusion
  100.8 0.1 broadcast_in_dim.41
  100.9 0.1 broadcast_in_dim.42
  100.9 0.1 pad_maximum_fusion.1
  101.1 26.2 %all_to_all.49 = bf16[16,4,640]{2,1,0:T(4,128)(2,1)S(1)} all-to-all(bf16[16,4,640]{2,1,0:T(4,128)(2,1)S(1)} %reshape.145), channel_id=1, replica_groups={{32,48,64,80,96,112,128,144,160,176,192,208,224,240,0,16},{33,49,65,81,..., dimensions={0} | all-to-all | bytes 163840 | tf_op jit(solution)/shard_map/all_to_all | solution.py:27
  127.3 0.1 fusion.12
  127.4 0.1 copy.23
  127.5 0.1 copy.24
  127.6 0.1 add_reduce_fusion.2
  127.8 0.1 divide_convert_fusion
  127.8 0.1 broadcast_in_dim.43
  127.9 0.1 broadcast_in_dim.44
  128.0 0.1 pad_maximum_fusion.2
  128.1 29.3 %all_to_all.50 = bf16[16,4,640]{2,1,0:T(4,128)(2,1)S(1)} all-to-all(bf16[16,4,640]{2,1,0:T(4,128)(2,1)S(1)} %broadcast_in_dim.45), channel_id=1, replica_groups={{32,48,64,80,96,112,128,144,160,176,192,208,224,240,0,16},{33,49,65,81,..., dimensions={0} | all-to-all | bytes 163840 | tf_op jit(solution)/shard_map/all_to_all | solution.py:27
  157.5 0.1 broadcast_in_dim.47
  157.5 10.8 %all_to_all.51 = bf16[8,64,640]{2,1,0:T(8,128)(2,1)S(1)} all-to-all(bf16[8,64,640]{2,1,0:T(8,128)(2,1)S(1)} %broadcast_in_dim.47), channel_id=1, replica_groups=mesh['dp'=4,'zh'=16,'zl'=2,'core'=2,'tensor'=4] {'dp','zl'}, dimensions={0} | all-to-all | bytes 1310720 | tf_op jit(solution)/shard_map/all_to_all | solution.py:27
  168.3 0.2 multiply_reduce_fusion
  168.5 0.1 reshape.147
  168.6 0.2 add_reduce_fusion.1
  168.8 0.1 add.153
  168.8 0.6 broadcast_in_dim.48
  169.5 7.7 %all-to-all-start.8 = ((f32[8,2,128]{2,1,0:T(2,128)}), f32[8,2,128]{2,1,0:T(2,128)S(1)}, u32[]{:S(2)}, u32[]{:S(2)}) async-start(f32[8,2,128]{2,1,0:T(2,128)} %broadcast_in_dim.48), calls=%async_computation.8 | async-start | bytes 16384 | tf_op jit(solution)/shard_map/all_to_all | solution.py:27
  177.1 2.0 %collective-permute-start.3 = (bf16[4,2,64,640]{3,2,1,0:T(8,128)(2,1)S(1)}, bf16[4,2,64,640]{3,2,1,0:T(8,128)(2,1)S(1)}, u32[]{:S(2)}, u32[]{:S(2)}) collective-permute-start(bf16[4,2,64,640]{3,2,1,0:T(8,128)(2,1)S(1)} %bitcast.36), channel_id=1, source_target_pairs={{0,4},{4,0},{1,5},{5,1},{2,6},{6,2},{3,7},{7,3},{8,12},{12,8},{9,1... | collective-permute-start | bytes 1966088 | tf_op jit(solution)/shard_map/ppermute | solution.py:157
  179.1 2.8 %all-to-all-done.8 = f32[8,2,128]{2,1,0:T(2,128)S(1)} async-done(((f32[8,2,128]{2,1,0:T(2,128)}), f32[8,2,128]{2,1,0:T(2,128)S(1)}, u32[]{:S(2)}, u32[]{:S(2)}) %all-to-all-start.8) | async-done | bytes 8224 | tf_op jit(solution)/shard_map/all_to_all | solution.py:27
  182.0 0.1 dynamic-slice_bitcast_fusion.1
  182.1 0.1 copy.26.own_norms_ref
  182.3 2.6 %shard_map.58 = (bf16[224,2048]{1,0:T(8,128)(2,1)}, bf16[224,2048]{1,0:T(8,128)(2,1)}, f32[4,2048]{1,0:T(4,128)}) custom-call(s32[1]{0:T(128)} %bitcast.core_ref, bf16[224,256]{1,0:T(8,128)(2,1)S(1)} %get-tuple-element.21.left_ref, f32[2,256]{1,0:T(2,128)S(1)} %pad_maximum_fusion.3.norms_ref, bf16[4,2,64,640]{3,2,1,0:T(8,128)(2,1)S(1)} %bitcast.38, ...), custom_call_target="tpu_custom_call" | custom-call | tf_op jit(solution)/shard_map/pallas_call | solution.py:82
  (31 shorter events, 0.5 us)
Async XLA Ops:
  0.6 0.8 copy-start
  2.1 54.3 %all-to-all-start = ((bf16[16,4,512]{2,1,0:T(4,128)(2,1)}), bf16[16,4,512]{2,1,0:T(4,128)(2,1)S(1)}, u32[]{:S(2)}, u32[]{:S(2)}) async-start(bf16[16,4,512]{2,1,0:T(4,128)(2,1)} %broadcast_in_dim.35), calls=%async_computation | async-start | bytes 131072 | tf_op jit(solution)/shard_map/all_to_all | solution.py:27
  37.6 18.6 %copy-start.1 = (bf16[1,224,2048]{2,1,0:T(8,128)(2,1)S(1)}, bf16[1,224,2048]{2,1,0:T(8,128)(2,1)}, u32[]{:S(2)}) copy-start(bf16[1,224,2048]{2,1,0:T(8,128)(2,1)} %param.4) | copy-start | bytes 2752516
  37.6 18.6 %copy-start.2 = (bf16[1,224,2048]{2,1,0:T(8,128)(2,1)S(1)}, bf16[1,224,2048]{2,1,0:T(8,128)(2,1)}, u32[]{:S(2)}) copy-start(bf16[1,224,2048]{2,1,0:T(8,128)(2,1)} %param.3) | copy-start | bytes 2752516
  39.4 10.7 %collective-permute-start = (bf16[224,512]{1,0:T(8,128)(2,1)S(1)}, bf16[224,512]{1,0:T(8,128)(2,1)S(1)}, u32[]{:S(2)}, u32[]{:S(2)}) collective-permute-start(bf16[224,512]{1,0:T(8,128)(2,1)S(1)} %get-tuple-element.17), channel_id=1, source_target_pairs={{0,256},{256,512},{512,768},{768,0},{1,257},{257,513},{513,769},{7... | collective-permute-start | bytes 688136 | tf_op jit(solution)/shard_map/ppermute | solution.py:123
  42.6 11.9 %collective-permute-start.1 = (bf16[224,512]{1,0:T(8,128)(2,1)S(1)}, bf16[224,512]{1,0:T(8,128)(2,1)S(1)}, u32[]{:S(2)}, u32[]{:S(2)}) collective-permute-start(bf16[224,512]{1,0:T(8,128)(2,1)S(1)} %get-tuple-element.18), channel_id=1, source_target_pairs={{0,512},{256,768},{512,0},{768,256},{1,513},{257,769},{513,1},{769... | collective-permute-start | bytes 688136 | tf_op jit(solution)/shard_map/ppermute | solution.py:123
  47.1 9.1 %collective-permute-start.2 = (bf16[224,512]{1,0:T(8,128)(2,1)S(1)}, bf16[224,512]{1,0:T(8,128)(2,1)S(1)}, u32[]{:S(2)}, u32[]{:S(2)}) collective-permute-start(bf16[224,512]{1,0:T(8,128)(2,1)S(1)} %get-tuple-element.19), channel_id=1, source_target_pairs={{0,768},{256,0},{512,256},{768,512},{1,769},{257,1},{513,257},{769... | collective-permute-start | bytes 688136 | tf_op jit(solution)/shard_map/ppermute | solution.py:123
  169.5 12.5 %all-to-all-start.8 = ((f32[8,2,128]{2,1,0:T(2,128)}), f32[8,2,128]{2,1,0:T(2,128)S(1)}, u32[]{:S(2)}, u32[]{:S(2)}) async-start(f32[8,2,128]{2,1,0:T(2,128)} %broadcast_in_dim.48), calls=%async_computation.8 | async-start | bytes 16384 | tf_op jit(solution)/shard_map/all_to_all | solution.py:27
  177.1 5.1 %collective-permute-start.3 = (bf16[4,2,64,640]{3,2,1,0:T(8,128)(2,1)S(1)}, bf16[4,2,64,640]{3,2,1,0:T(8,128)(2,1)S(1)}, u32[]{:S(2)}, u32[]{:S(2)}) collective-permute-start(bf16[4,2,64,640]{3,2,1,0:T(8,128)(2,1)S(1)} %bitcast.36), channel_id=1, source_target_pairs={{0,4},{4,0},{1,5},{5,1},{2,6},{6,2},{3,7},{7,3},{8,12},{12,8},{9,1... | collective-permute-start | bytes 1966088 | tf_op jit(solution)/shard_map/ppermute | solution.py:157

commit v4 on v3

--- a/solution.py
+++ b/solution.py
@@ -110,9 +110,10 @@
     part = width // replicas
     rank = own_rows * far * near
     half = rank // 2
+    early, late = 11 * far // 16, 5 * far // 16
 
     own_basis = lax.dynamic_slice_in_dim(basis, me * part, part, 1).astype(bf16)
-    far_basis = gather(own_basis, "zh", far // 2).reshape(far * own_rows, part)
+    far_basis = gather(own_basis, "zh", early).reshape(far * own_rows, part)
 
     def column_block(index):
         first = lax.dynamic_slice_in_dim(momentum[0], index * part, part, 1).astype(f32)
@@ -146,13 +147,13 @@
     right_near = jnp.sum(packed[..., :part].astype(f32), axis=0)
     squares_near = jnp.sum(from_lanes(packed[..., part:]), axis=0)
     packed = jnp.concatenate([right_near.astype(bf16), pair_lanes(squares_near)], axis=1)
-    packed = exchange(packed.reshape(far, own_rows, part + LANES), "zh", far // 8)
+    packed = exchange(packed.reshape(far, own_rows, part + LANES), "zh", late)
     right_un = jnp.sum(packed[..., :part].astype(f32), axis=0)
     norms = jnp.sqrt(jnp.sum(from_lanes(packed[..., part:]), axis=0) + epsilon)
     right_own = (right_un / norms[:, None]).astype(bf16)
 
     packed = jnp.concatenate([right_own, pair_lanes(norms)], axis=1)
-    packed = gather(packed, "zh", far // 8).reshape(far * own_rows, part + LANES)
+    packed = gather(packed, "zh", late).reshape(far * own_rows, part + LANES)
     packed = gather(packed, ("dp", "zl")).reshape(replicas, 2, half // 2, part + LANES)
     other = lax.ppermute(packed, "core", [(0, 1), (1, 0)])
 
@@ -163,7 +164,7 @@
     both = both.reshape(2, -1, 2, half)
     right_norms = jnp.sqrt(jnp.sum(both[:, :, 1], axis=1) + epsilon).reshape(rank)
     norms = jnp.stack([both[:, 0, 0].reshape(rank), right_norms])
-    place = (lax.axis_index("zh") + far // 2) % far
+    place = (lax.axis_index("zh") + far - early) % far
     pair = lax.axis_index("zl")
     gathered, right_norms = lax.optimization_barrier((packed, right_norms))
     own = lax.dynamic_slice(

time: 186 us -> 182 us (0.978)
  starting transfers between devices: 55.9 us -> 47.6 us
  blocking collectives: 109 us -> 114 us
    all_to_all x2, starting transfers between devices: 43.2 us -> 34.8 us  [exchange(): lax.all_to_all(blocks, axes, 0, 0, axis_index_groups=groups, tiled=False)]
    all_to_all x7, blocking collectives: 109 us -> 114 us  [exchange(): lax.all_to_all(blocks, axes, 0, 0, axis_index_groups=groups, tiled=False)]
where the time goes in v4:
time: 182 us; the launch traced here: 181 us
  blocking collectives  114 us (63%)
  starting transfers between devices  47.6 us (26%)
  waiting for transfers between devices  8.93 us (5%)
  local copies, waits for them, and re-layouts  3.46 us (2%)
  other arithmetic  3.22 us (2%)
  Pallas kernels  2.63 us (1%)
    all_to_all x7, blocking collectives, exchange(): lax.all_to_all(blocks, axes, 0, 0, axis_index_groups=groups, tiled=False)  114 us
    all_to_all x2, starting transfers between devices, exchange(): lax.all_to_all(blocks, axes, 0, 0, axis_index_groups=groups, tiled=False)  34.8 us
    ppermute x3, starting transfers between devices, body(): lax.ppermute(column_block((me + k) % replicas), 'dp', [(i, (i + k) % repl...  10.7 us
    ppermute x3, waiting for transfers between devices, body(): lax.ppermute(column_block((me + k) % replicas), 'dp', [(i, (i + k) % repl...  6.08 us
  transfers between devices with their start and end apart: 6, of which 3 were waited for; matrix products, arithmetic and copies ran while one was open for 1% of the time, Pallas kernels for 0%

profile of v4, /device:TPU:1, one launch (start us, length us, event | category | flops | bytes accessed | tf_op | source)
XLA Modules:
  0.0 180.9 jit_solution(17305281281518523841)
XLA Ops:
  0.7 0.7 copy-done
  1.4 0.7 broadcast_in_dim.35
  2.1 29.2 %all-to-all-start = ((bf16[16,4,512]{2,1,0:T(4,128)(2,1)}), bf16[16,4,512]{2,1,0:T(4,128)(2,1)S(1)}, u32[]{:S(2)}, u32[]{:S(2)}) async-start(bf16[16,4,512]{2,1,0:T(4,128)(2,1)} %broadcast_in_dim.35), calls=%async_computation | async-start | bytes 131072 | tf_op jit(solution)/shard_map/all_to_all | solution.py:27
  31.3 1.7 fusion.5
  33.0 3.2 %collective-permute-start = (bf16[224,512]{1,0:T(8,128)(2,1)S(1)}, bf16[224,512]{1,0:T(8,128)(2,1)S(1)}, u32[]{:S(2)}, u32[]{:S(2)}) collective-permute-start(bf16[224,512]{1,0:T(8,128)(2,1)S(1)} %get-tuple-element.17), channel_id=1, source_target_pairs={{0,256},{256,512},{512,768},{768,0},{1,257},{257,513},{513,769},{7... | collective-permute-start | bytes 688136 | tf_op jit(solution)/shard_map/ppermute | solution.py:124
  36.2 4.5 %collective-permute-start.1 = (bf16[224,512]{1,0:T(8,128)(2,1)S(1)}, bf16[224,512]{1,0:T(8,128)(2,1)S(1)}, u32[]{:S(2)}, u32[]{:S(2)}) collective-permute-start(bf16[224,512]{1,0:T(8,128)(2,1)S(1)} %get-tuple-element.18), channel_id=1, source_target_pairs={{0,512},{256,768},{512,0},{768,256},{1,513},{257,769},{513,1},{769... | collective-permute-start | bytes 688136 | tf_op jit(solution)/shard_map/ppermute | solution.py:124
  40.7 3.0 %collective-permute-start.2 = (bf16[224,512]{1,0:T(8,128)(2,1)S(1)}, bf16[224,512]{1,0:T(8,128)(2,1)S(1)}, u32[]{:S(2)}, u32[]{:S(2)}) collective-permute-start(bf16[224,512]{1,0:T(8,128)(2,1)S(1)} %get-tuple-element.19), channel_id=1, source_target_pairs={{0,768},{256,0},{512,256},{768,512},{1,769},{257,1},{513,257},{769... | collective-permute-start | bytes 688136 | tf_op jit(solution)/shard_map/ppermute | solution.py:124
  43.7 4.4 %collective-permute-done.1 = bf16[224,512]{1,0:T(8,128)(2,1)S(1)} collective-permute-done((bf16[224,512]{1,0:T(8,128)(2,1)S(1)}, bf16[224,512]{1,0:T(8,128)(2,1)S(1)}, u32[]{:S(2)}, u32[]{:S(2)}) %collective-permute-start.1) | collective-permute-done | bytes 229408 | tf_op jit(solution)/shard_map/ppermute | solution.py:124
  48.1 1.7 collective-permute-done.2
  49.8 0.2 fusion.3
  50.1 9.2 %all_to_all.45 = bf16[4,64,512]{2,1,0:T(8,128)(2,1)S(1)} all-to-all(bf16[4,64,512]{2,1,0:T(8,128)(2,1)S(1)} %broadcast_in_dim.36), channel_id=1, replica_groups=mesh['dp'=4,'zh'=16,'zl'=2,'core'=2,'tensor'=4] {'core','zl'}, dimensions={0} | all-to-all | bytes 524288 | tf_op jit(solution)/shard_map/all_to_all | solution.py:27
  59.2 0.2 convolution_convert_fusion.1
  59.5 11.3 %all_to_all.46 = bf16[4,224,256]{2,1,0:T(8,128)(2,1)S(1)} all-to-all(bf16[4,224,256]{2,1,0:T(8,128)(2,1)S(1)} %broadcast_in_dim.37), channel_id=1, replica_groups=mesh['dp'=4,'zh'=16,'zl'=2,'core'=2,'tensor'=4] {'tensor'}, dimensions={0} | all-to-all | bytes 917504 | tf_op jit(solution)/shard_map/all_to_all | solution.py:27
  70.8 0.1 reduce_sum.87
  70.9 10.5 %all_to_all.47 = bf16[4,224,256]{2,1,0:T(8,128)(2,1)S(1)} all-to-all(bf16[4,224,256]{2,1,0:T(8,128)(2,1)S(1)} %broadcast_in_dim.38), channel_id=1, replica_groups=mesh['dp'=4,'zh'=16,'zl'=2,'core'=2,'tensor'=4] {'dp'}, dimensions={0} | all-to-all | bytes 917504 | tf_op jit(solution)/shard_map/all_to_all | solution.py:27
  81.5 0.1 convert_reduce_fusion
  81.6 0.2 convolution_convert_fusion
  81.8 0.1 broadcast_in_dim.39
  81.9 0.1 broadcast_in_dim.40
  82.1 0.1 pad_maximum_fusion
  82.2 12.0 %all_to_all.48 = bf16[4,64,640]{2,1,0:T(8,128)(2,1)S(1)} all-to-all(bf16[4,64,640]{2,1,0:T(8,128)(2,1)S(1)} %bitcast.41), channel_id=1, replica_groups=mesh['dp'=4,'zh'=16,'zl'=2,'core'=2,'tensor'=4] {'core','zl'}, dimensions={0} | all-to-all | bytes 655360 | tf_op jit(solution)/shard_map/all_to_all | solution.py:27
  94.2 0.2 add_reduce_fusion
  94.4 0.1 broadcast_in_dim.41
  94.5 0.1 broadcast_in_dim.42
  94.6 0.1 pad_maximum_fusion.1
  94.7 28.4 %all_to_all.49 = bf16[16,4,640]{2,1,0:T(4,128)(2,1)S(1)} all-to-all(bf16[16,4,640]{2,1,0:T(4,128)(2,1)S(1)} %reshape.145), channel_id=1, replica_groups={{80,96,112,128,144,160,176,192,208,224,240,0,16,32,48,64},{81,97,113,12..., dimensions={0} | all-to-all | bytes 163840 | tf_op jit(solution)/shard_map/all_to_all | solution.py:27
  123.1 0.1 fusion.12
  123.2 0.1 copy.23
  123.3 0.1 copy.24
  123.4 0.1 add_reduce_fusion.2
  123.6 0.1 divide_convert_fusion
  123.6 0.1 broadcast_in_dim.43
  123.7 0.1 broadcast_in_dim.44
  123.8 0.1 pad_maximum_fusion.2
  123.9 29.2 %all_to_all.50 = bf16[16,4,640]{2,1,0:T(4,128)(2,1)S(1)} all-to-all(bf16[16,4,640]{2,1,0:T(4,128)(2,1)S(1)} %broadcast_in_dim.45), channel_id=1, replica_groups={{80,96,112,128,144,160,176,192,208,224,240,0,16,32,48,64},{81,97,113,12..., dimensions={0} | all-to-all | bytes 163840 | tf_op jit(solution)/shard_map/all_to_all | solution.py:27
  153.2 0.1 broadcast_in_dim.47
  153.2 13.1 %all_to_all.51 = bf16[8,64,640]{2,1,0:T(8,128)(2,1)S(1)} all-to-all(bf16[8,64,640]{2,1,0:T(8,128)(2,1)S(1)} %broadcast_in_dim.47), channel_id=1, replica_groups=mesh['dp'=4,'zh'=16,'zl'=2,'core'=2,'tensor'=4] {'dp','zl'}, dimensions={0} | all-to-all | bytes 1310720 | tf_op jit(solution)/shard_map/all_to_all | solution.py:27
  166.4 0.2 multiply_reduce_fusion
  166.6 0.1 reshape.147
  166.7 0.2 add_reduce_fusion.1
  166.8 0.1 add.154
  166.9 0.6 broadcast_in_dim.48
  167.5 5.6 %all-to-all-start.8 = ((f32[8,2,128]{2,1,0:T(2,128)}), f32[8,2,128]{2,1,0:T(2,128)S(1)}, u32[]{:S(2)}, u32[]{:S(2)}) async-start(f32[8,2,128]{2,1,0:T(2,128)} %broadcast_in_dim.48), calls=%async_computation.8 | async-start | bytes 16384 | tf_op jit(solution)/shard_map/all_to_all | solution.py:27
  173.2 2.0 %collective-permute-start.3 = (bf16[4,2,64,640]{3,2,1,0:T(8,128)(2,1)S(1)}, bf16[4,2,64,640]{3,2,1,0:T(8,128)(2,1)S(1)}, u32[]{:S(2)}, u32[]{:S(2)}) collective-permute-start(bf16[4,2,64,640]{3,2,1,0:T(8,128)(2,1)S(1)} %bitcast.36), channel_id=1, source_target_pairs={{0,4},{4,0},{1,5},{5,1},{2,6},{6,2},{3,7},{7,3},{8,12},{12,8},{9,1... | collective-permute-start | bytes 1966088 | tf_op jit(solution)/shard_map/ppermute | solution.py:158
  175.2 2.8 %all-to-all-done.8 = f32[8,2,128]{2,1,0:T(2,128)S(1)} async-done(((f32[8,2,128]{2,1,0:T(2,128)}), f32[8,2,128]{2,1,0:T(2,128)S(1)}, u32[]{:S(2)}, u32[]{:S(2)}) %all-to-all-start.8) | async-done | bytes 8224 | tf_op jit(solution)/shard_map/all_to_all | solution.py:27
  178.1 0.1 dynamic-slice_bitcast_fusion.1
  178.2 0.1 copy.26.own_norms_ref
  178.3 2.6 %shard_map.58 = (bf16[224,2048]{1,0:T(8,128)(2,1)}, bf16[224,2048]{1,0:T(8,128)(2,1)}, f32[4,2048]{1,0:T(4,128)}) custom-call(s32[1]{0:T(128)} %bitcast.core_ref, bf16[224,256]{1,0:T(8,128)(2,1)S(1)} %get-tuple-element.21.left_ref, f32[2,256]{1,0:T(2,128)S(1)} %pad_maximum_fusion.3.norms_ref, bf16[4,2,64,640]{3,2,1,0:T(8,128)(2,1)S(1)} %bitcast.38, ...), custom_call_target="tpu_custom_call" | custom-call | tf_op jit(solution)/shard_map/pallas_call | solution.py:82
  (31 shorter events, 0.5 us)
Async XLA Ops:
  0.6 0.8 copy-start
  2.1 48.0 %all-to-all-start = ((bf16[16,4,512]{2,1,0:T(4,128)(2,1)}), bf16[16,4,512]{2,1,0:T(4,128)(2,1)S(1)}, u32[]{:S(2)}, u32[]{:S(2)}) async-start(bf16[16,4,512]{2,1,0:T(4,128)(2,1)} %broadcast_in_dim.35), calls=%async_computation | async-start | bytes 131072 | tf_op jit(solution)/shard_map/all_to_all | solution.py:27
  31.2 18.6 %copy-start.1 = (bf16[1,224,2048]{2,1,0:T(8,128)(2,1)S(1)}, bf16[1,224,2048]{2,1,0:T(8,128)(2,1)}, u32[]{:S(2)}) copy-start(bf16[1,224,2048]{2,1,0:T(8,128)(2,1)} %param.4) | copy-start | bytes 2752516
  31.2 18.6 %copy-start.2 = (bf16[1,224,2048]{2,1,0:T(8,128)(2,1)S(1)}, bf16[1,224,2048]{2,1,0:T(8,128)(2,1)}, u32[]{:S(2)}) copy-start(bf16[1,224,2048]{2,1,0:T(8,128)(2,1)} %param.3) | copy-start | bytes 2752516
  33.0 10.7 %collective-permute-start = (bf16[224,512]{1,0:T(8,128)(2,1)S(1)}, bf16[224,512]{1,0:T(8,128)(2,1)S(1)}, u32[]{:S(2)}, u32[]{:S(2)}) collective-permute-start(bf16[224,512]{1,0:T(8,128)(2,1)S(1)} %get-tuple-element.17), channel_id=1, source_target_pairs={{0,256},{256,512},{512,768},{768,0},{1,257},{257,513},{513,769},{7... | collective-permute-start | bytes 688136 | tf_op jit(solution)/shard_map/ppermute | solution.py:124
  36.2 11.9 %collective-permute-start.1 = (bf16[224,512]{1,0:T(8,128)(2,1)S(1)}, bf16[224,512]{1,0:T(8,128)(2,1)S(1)}, u32[]{:S(2)}, u32[]{:S(2)}) collective-permute-start(bf16[224,512]{1,0:T(8,128)(2,1)S(1)} %get-tuple-element.18), channel_id=1, source_target_pairs={{0,512},{256,768},{512,0},{768,256},{1,513},{257,769},{513,1},{769... | collective-permute-start | bytes 688136 | tf_op jit(solution)/shard_map/ppermute | solution.py:124
  40.7 9.1 %collective-permute-start.2 = (bf16[224,512]{1,0:T(8,128)(2,1)S(1)}, bf16[224,512]{1,0:T(8,128)(2,1)S(1)}, u32[]{:S(2)}, u32[]{:S(2)}) collective-permute-start(bf16[224,512]{1,0:T(8,128)(2,1)S(1)} %get-tuple-element.19), channel_id=1, source_target_pairs={{0,768},{256,0},{512,256},{768,512},{1,769},{257,1},{513,257},{769... | collective-permute-start | bytes 688136 | tf_op jit(solution)/shard_map/ppermute | solution.py:124
  167.5 10.5 %all-to-all-start.8 = ((f32[8,2,128]{2,1,0:T(2,128)}), f32[8,2,128]{2,1,0:T(2,128)S(1)}, u32[]{:S(2)}, u32[]{:S(2)}) async-start(f32[8,2,128]{2,1,0:T(2,128)} %broadcast_in_dim.48), calls=%async_computation.8 | async-start | bytes 16384 | tf_op jit(solution)/shard_map/all_to_all | solution.py:27
  173.2 5.1 %collective-permute-start.3 = (bf16[4,2,64,640]{3,2,1,0:T(8,128)(2,1)S(1)}, bf16[4,2,64,640]{3,2,1,0:T(8,128)(2,1)S(1)}, u32[]{:S(2)}, u32[]{:S(2)}) collective-permute-start(bf16[4,2,64,640]{3,2,1,0:T(8,128)(2,1)S(1)} %bitcast.36), channel_id=1, source_target_pairs={{0,4},{4,0},{1,5},{5,1},{2,6},{6,2},{3,7},{7,3},{8,12},{12,8},{9,1... | collective-permute-start | bytes 1966088 | tf_op jit(solution)/shard_map/ppermute | solution.py:158

commit v5 on v4

--- a/solution.py
+++ b/solution.py
@@ -32,19 +32,15 @@
     return exchange(jnp.broadcast_to(block[None], (count,) + block.shape), axes, first)
 
 
-def pair_lanes(values):
+def split_rows(values):
     high = lax.reduce_precision(values, 8, 7)
-    low = (values - high).astype(bf16)
-    high = high.astype(bf16)
-    rows = values.shape[0]
-    half = (rows, LANES // 2)
-    return jnp.concatenate(
-        [jnp.broadcast_to(high[:, None], half), jnp.broadcast_to(low[:, None], half)], axis=1
-    )
+    return jnp.concatenate([high, values - high]).astype(bf16).reshape(-1, LANES)
 
 
-def from_lanes(lanes):
-    return lanes[..., 0].astype(f32) + lanes[..., LANES // 2].astype(f32)
+def joined(rows):
+    total = jnp.sum(rows.astype(f32), axis=0)
+    half = total.shape[0] // 2
+    return (total[:half] + total[half:]).reshape(-1)
 
 
 def finish_kernel(
@@ -75,7 +71,7 @@
 def finish(core, left, norms, mine, other, momentum, gradient, own, own_norms, scale):
     replicas, pair, block, _ = mine.shape
     rows, rank = left.shape
-    part = mine.shape[3] - LANES
+    part = mine.shape[3]
     tile = pl.BlockSpec((rows, part), lambda d: (0, d))
     right = pl.BlockSpec((None, pair, block, part), lambda d: (d, 0, 0, 0))
     wide = jax.ShapeDtypeStruct((rows, replicas * part), bf16)
@@ -130,7 +126,14 @@
     for piece in pieces:
         total = total + piece.astype(f32)
     mean_h = (total / replicas).astype(bf16)
-    far_basis, mean_h = lax.optimization_barrier((far_basis, mean_h))
+    zh, pair = lax.axis_index("zh"), lax.axis_index("zl")
+    summed = (lax.axis_index(NEAR) * far + (zh + far - late) % far) * own_rows
+    place = (zh + far - early) % far * own_rows
+    first = core * half + pair * (half // 2) + place
+    indices = [index.astype(jnp.uint32) for index in (summed, place, first, pair)]
+    far_basis, mean_h, *indices = lax.optimization_barrier((far_basis, mean_h, *indices))
+    summed, place, first, pair = indices
+    zero = jnp.uint32(0)
     basis_h = gather(far_basis, NEAR).reshape(rank, part)
 
     left = lax.dot_general(basis_h, mean_h, (((1,), (1,)), ((), ())), preferred_element_type=f32).T
@@ -142,35 +145,34 @@
     right_term = lax.dot_general(
         left_h, mean_h, (((0,), (0,)), ((), ())), preferred_element_type=f32
     ).astype(bf16)
-    packed = jnp.concatenate([right_term, pair_lanes(squares)], axis=1)
+    def with_squares(right, values):
+        lanes = jnp.tile(split_rows(values), (right.shape[0] // own_rows, 1))
+        return jnp.concatenate([right, lanes], axis=1)
+
+    packed = with_squares(right_term, squares)
     packed = exchange(packed.reshape(near, rank // near, part + LANES), NEAR)
     right_near = jnp.sum(packed[..., :part].astype(f32), axis=0)
-    squares_near = jnp.sum(from_lanes(packed[..., part:]), axis=0)
-    packed = jnp.concatenate([right_near.astype(bf16), pair_lanes(squares_near)], axis=1)
+    packed = with_squares(right_near.astype(bf16), joined(packed[:, :own_rows, part:]))
     packed = exchange(packed.reshape(far, own_rows, part + LANES), "zh", late)
     right_un = jnp.sum(packed[..., :part].astype(f32), axis=0)
-    norms = jnp.sqrt(jnp.sum(from_lanes(packed[..., part:]), axis=0) + epsilon)
+    left_norms = jnp.sqrt(joined(packed[..., part:]) + epsilon)
+    norms = lax.dynamic_slice(left_norms, (summed,), (own_rows,))
     right_own = (right_un / norms[:, None]).astype(bf16)
 
-    packed = jnp.concatenate([right_own, pair_lanes(norms)], axis=1)
-    packed = gather(packed, "zh", late).reshape(far * own_rows, part + LANES)
-    packed = gather(packed, ("dp", "zl")).reshape(replicas, 2, half // 2, part + LANES)
+    packed = gather(right_own, "zh", late).reshape(far * own_rows, part)
+    packed = gather(packed, ("dp", "zl")).reshape(replicas, 2, half // 2, part)
     other = lax.ppermute(packed, "core", [(0, 1), (1, 0)])
 
-    right_wide = packed[..., :part].astype(f32)
+    right_wide = packed.astype(f32)
     right_squares = jnp.sum(right_wide * right_wide, axis=(0, 3)).reshape(1, half)
-    left_norms = from_lanes(packed[0, ..., part:]).reshape(1, half)
-    both = gather(jnp.concatenate([left_norms, right_squares]), ("core", "tensor"))
-    both = both.reshape(2, -1, 2, half)
-    right_norms = jnp.sqrt(jnp.sum(both[:, :, 1], axis=1) + epsilon).reshape(rank)
-    norms = jnp.stack([both[:, 0, 0].reshape(rank), right_norms])
-    place = (lax.axis_index("zh") + far - early) % far
-    pair = lax.axis_index("zl")
+    right_squares = gather(right_squares, ("core", "tensor")).reshape(2, -1, half)
+    right_norms = jnp.sqrt(jnp.sum(right_squares, axis=1) + epsilon).reshape(rank)
+    norms = jnp.stack([left_norms, right_norms])
+
     gathered, right_norms = lax.optimization_barrier((packed, right_norms))
     own = lax.dynamic_slice(
-        gathered, (0, pair, place * own_rows, 0), (replicas, 1, own_rows, part)
+        gathered, (zero, pair, place, zero), (replicas, 1, own_rows, part)
     )[:, 0]
-    first = core * half + pair * (half // 2) + place * own_rows
     own_norms = lax.dynamic_slice(right_norms, (first,), (own_rows,))[:, None]
     momentum_next, update, basis_next = finish(
         core, left_h, norms, packed, other, momentum[0], gradient[0], own, own_norms,

time: 182 us -> 176 us (0.967)
  blocking collectives: 114 us -> 110 us
    all_to_all x7, blocking collectives: 114 us -> 110 us  [exchange(): lax.all_to_all(blocks, axes, 0, 0, axis_index_groups=groups, tiled=False)]
where the time goes in v5:
time: 176 us
  blocking collectives  110 us (62%)
  starting transfers between devices  47.7 us (27%)
  waiting for transfers between devices  8.52 us (5%)
  local copies, waits for them, and re-layouts  2.65 us (2%)
  other arithmetic  2.62 us (1%)
  Pallas kernels  2.57 us (1%)
    all_to_all x7, blocking collectives, exchange(): lax.all_to_all(blocks, axes, 0, 0, axis_index_groups=groups, tiled=False)  110 us
    all_to_all x2, starting transfers between devices, exchange(): lax.all_to_all(blocks, axes, 0, 0, axis_index_groups=groups, tiled=False)  35 us
    ppermute x3, starting transfers between devices, body(): lax.ppermute(column_block((me + k) % replicas), 'dp', [(i, (i + k) % repl...  10.7 us
    ppermute x3, waiting for transfers between devices, body(): lax.ppermute(column_block((me + k) % replicas), 'dp', [(i, (i + k) % repl...  6.05 us
  transfers between devices with their start and end apart: 6, of which 3 were waited for; matrix products, arithmetic and copies ran while one was open for 1% of the time, Pallas kernels for 0%

profile of v5, /device:TPU:1, one launch (start us, length us, event | category | flops | bytes accessed | tf_op | source)
XLA Modules:
  0.0 175.7 jit_solution(17850347431896711112)
XLA Ops:
  0.6 0.0 copy-start
  0.7 0.7 copy-done
  1.4 0.7 broadcast_in_dim.25
  2.1 29.2 %all-to-all-start = ((bf16[16,4,512]{2,1,0:T(4,128)(2,1)}), bf16[16,4,512]{2,1,0:T(4,128)(2,1)S(1)}, u32[]{:S(2)}, u32[]{:S(2)}) async-start(bf16[16,4,512]{2,1,0:T(4,128)(2,1)} %broadcast_in_dim.25), calls=%async_computation | async-start | bytes 131072 | tf_op jit(solution)/shard_map/all_to_all | solution.py:27
  31.2 0.0 copy-start.1
  31.2 0.0 copy-start.2
  31.3 1.7 fusion.5
  33.0 3.2 %collective-permute-start = (bf16[224,512]{1,0:T(8,128)(2,1)S(1)}, bf16[224,512]{1,0:T(8,128)(2,1)S(1)}, u32[]{:S(2)}, u32[]{:S(2)}) collective-permute-start(bf16[224,512]{1,0:T(8,128)(2,1)S(1)} %get-tuple-element.25), channel_id=1, source_target_pairs={{0,256},{256,512},{512,768},{768,0},{1,257},{257,513},{513,769},{7... | collective-permute-start | bytes 688136 | tf_op jit(solution)/shard_map/ppermute | solution.py:120
  36.2 4.5 %collective-permute-start.1 = (bf16[224,512]{1,0:T(8,128)(2,1)S(1)}, bf16[224,512]{1,0:T(8,128)(2,1)S(1)}, u32[]{:S(2)}, u32[]{:S(2)}) collective-permute-start(bf16[224,512]{1,0:T(8,128)(2,1)S(1)} %get-tuple-element.26), channel_id=1, source_target_pairs={{0,512},{256,768},{512,0},{768,256},{1,513},{257,769},{513,1},{769... | collective-permute-start | bytes 688136 | tf_op jit(solution)/shard_map/ppermute | solution.py:120
  40.7 3.0 %collective-permute-start.2 = (bf16[224,512]{1,0:T(8,128)(2,1)S(1)}, bf16[224,512]{1,0:T(8,128)(2,1)S(1)}, u32[]{:S(2)}, u32[]{:S(2)}) collective-permute-start(bf16[224,512]{1,0:T(8,128)(2,1)S(1)} %get-tuple-element.27), channel_id=1, source_target_pairs={{0,768},{256,0},{512,256},{768,512},{1,769},{257,1},{513,257},{769... | collective-permute-start | bytes 688136 | tf_op jit(solution)/shard_map/ppermute | solution.py:120
  43.8 0.0 collective-permute-done
  43.8 4.3 %collective-permute-done.1 = bf16[224,512]{1,0:T(8,128)(2,1)S(1)} collective-permute-done((bf16[224,512]{1,0:T(8,128)(2,1)S(1)}, bf16[224,512]{1,0:T(8,128)(2,1)S(1)}, u32[]{:S(2)}, u32[]{:S(2)}) %collective-permute-start.1) | collective-permute-done | bytes 229408 | tf_op jit(solution)/shard_map/ppermute | solution.py:120
  48.1 1.7 collective-permute-done.2
  49.8 0.0 copy-done.1
  49.8 0.0 copy-done.2
  49.8 0.2 fusion.3
  50.0 0.0 all-to-all-done
  50.1 9.2 %all_to_all.45 = bf16[4,64,512]{2,1,0:T(8,128)(2,1)S(1)} all-to-all(bf16[4,64,512]{2,1,0:T(8,128)(2,1)S(1)} %broadcast_in_dim.26), channel_id=1, replica_groups=mesh['dp'=4,'zh'=16,'zl'=2,'core'=2,'tensor'=4] {'core','zl'}, dimensions={0} | all-to-all | bytes 524288 | tf_op jit(solution)/shard_map/all_to_all | solution.py:27
  59.2 0.2 convolution_convert_fusion.1
  59.5 11.3 %all_to_all.46 = bf16[4,224,256]{2,1,0:T(8,128)(2,1)S(1)} all-to-all(bf16[4,224,256]{2,1,0:T(8,128)(2,1)S(1)} %broadcast_in_dim.27), channel_id=1, replica_groups=mesh['dp'=4,'zh'=16,'zl'=2,'core'=2,'tensor'=4] {'tensor'}, dimensions={0} | all-to-all | bytes 917504 | tf_op jit(solution)/shard_map/all_to_all | solution.py:27
  70.8 0.1 reduce_sum.96
  70.9 10.5 %all_to_all.47 = bf16[4,224,256]{2,1,0:T(8,128)(2,1)S(1)} all-to-all(bf16[4,224,256]{2,1,0:T(8,128)(2,1)S(1)} %broadcast_in_dim.28), channel_id=1, replica_groups=mesh['dp'=4,'zh'=16,'zl'=2,'core'=2,'tensor'=4] {'dp'}, dimensions={0} | all-to-all | bytes 917504 | tf_op jit(solution)/shard_map/all_to_all | solution.py:27
  81.5 0.1 convert_reduce_fusion
  81.6 0.2 convolution_convert_fusion
  81.9 12.0 %all_to_all.48 = bf16[4,64,640]{2,1,0:T(8,128)(2,1)S(1)} all-to-all(bf16[4,64,640]{2,1,0:T(8,128)(2,1)S(1)} %pad_maximum_fusion), channel_id=1, replica_groups=mesh['dp'=4,'zh'=16,'zl'=2,'core'=2,'tensor'=4] {'core','zl'}, dimensions={0} | all-to-all | bytes 655360 | tf_op jit(solution)/shard_map/all_to_all | solution.py:27
  94.1 28.4 %all_to_all.49 = bf16[16,4,640]{2,1,0:T(4,128)(2,1)S(1)} all-to-all(bf16[16,4,640]{2,1,0:T(4,128)(2,1)S(1)} %pad_maximum_fusion.1), channel_id=1, replica_groups={{80,96,112,128,144,160,176,192,208,224,240,0,16,32,48,64},{81,97,113,12..., dimensions={0} | all-to-all | bytes 163840 | tf_op jit(solution)/shard_map/all_to_all | solution.py:27
  122.6 0.1 dynamic_slice.45
  122.7 0.1 divide_convert_fusion
  122.8 27.8 %all_to_all.50 = bf16[16,4,512]{2,1,0:T(4,128)(2,1)S(1)} all-to-all(bf16[16,4,512]{2,1,0:T(4,128)(2,1)S(1)} %broadcast_in_dim.29), channel_id=1, replica_groups={{80,96,112,128,144,160,176,192,208,224,240,0,16,32,48,64},{81,97,113,12..., dimensions={0} | all-to-all | bytes 131072 | tf_op jit(solution)/shard_map/all_to_all | solution.py:27
  150.7 11.0 %all_to_all.51 = bf16[8,64,512]{2,1,0:T(8,128)(2,1)S(1)} all-to-all(bf16[8,64,512]{2,1,0:T(8,128)(2,1)S(1)} %broadcast_in_dim.61), channel_id=1, replica_groups=mesh['dp'=4,'zh'=16,'zl'=2,'core'=2,'tensor'=4] {'dp','zl'}, dimensions={0} | all-to-all | bytes 1048576 | tf_op jit(solution)/shard_map/all_to_all | solution.py:27
  161.7 0.2 multiply_reduce_fusion
  161.9 0.1 broadcast_in_dim.62
  162.0 0.6 broadcast_in_dim.63
  162.6 5.8 %all-to-all-start.8 = ((f32[8,1,128]{2,1,0:T(1,128)}), f32[8,1,128]{2,1,0:T(1,128)S(1)}, u32[]{:S(2)}, u32[]{:S(2)}) async-start(f32[8,1,128]{2,1,0:T(1,128)} %broadcast_in_dim.63), calls=%async_computation.8 | async-start | bytes 8192 | tf_op jit(solution)/shard_map/all_to_all | solution.py:27
  168.4 2.0 %collective-permute-start.3 = (bf16[4,2,64,512]{3,2,1,0:T(8,128)(2,1)S(1)}, bf16[4,2,64,512]{3,2,1,0:T(8,128)(2,1)S(1)}, u32[]{:S(2)}, u32[]{:S(2)}) collective-permute-start(bf16[4,2,64,512]{3,2,1,0:T(8,128)(2,1)S(1)} %bitcast.38), channel_id=1, source_target_pairs={{0,4},{4,0},{1,5},{5,1},{2,6},{6,2},{3,7},{7,3},{8,12},{12,8},{9,1... | collective-permute-start | bytes 1572872 | tf_op jit(solution)/shard_map/ppermute | solution.py:164
  170.4 2.5 %all-to-all-done.8 = f32[8,1,128]{2,1,0:T(1,128)S(1)} async-done(((f32[8,1,128]{2,1,0:T(1,128)}), f32[8,1,128]{2,1,0:T(1,128)S(1)}, u32[]{:S(2)}, u32[]{:S(2)}) %all-to-all-start.8) | async-done | bytes 4128 | tf_op jit(solution)/shard_map/all_to_all | solution.py:27
  172.9 0.1 dynamic-slice_bitcast_fusion.1
  173.0 0.1 copy.22.own_norms_ref
  173.1 0.0 collective-permute-done.3.other_ref
  173.1 2.6 %shard_map.58 = (bf16[224,2048]{1,0:T(8,128)(2,1)}, bf16[224,2048]{1,0:T(8,128)(2,1)}, f32[4,2048]{1,0:T(4,128)}) custom-call(s32[1]{0:T(128)} %bitcast.core_ref, bf16[224,256]{1,0:T(8,128)(2,1)S(1)} %get-tuple-element.29.left_ref, f32[2,256]{1,0:T(2,128)S(1)} %pad_maximum_fusion.2.norms_ref, bf16[4,2,64,512]{3,2,1,0:T(8,128)(2,1)S(1)} %bitcast.40, ...), custom_call_target="tpu_custom_call" | custom-call | tf_op jit(solution)/shard_map/pallas_call | solution.py:78
  (31 shorter events, 0.6 us)
Async XLA Ops:
  0.6 0.8 copy-start
  2.1 48.0 %all-to-all-start = ((bf16[16,4,512]{2,1,0:T(4,128)(2,1)}), bf16[16,4,512]{2,1,0:T(4,128)(2,1)S(1)}, u32[]{:S(2)}, u32[]{:S(2)}) async-start(bf16[16,4,512]{2,1,0:T(4,128)(2,1)} %broadcast_in_dim.25), calls=%async_computation | async-start | bytes 131072 | tf_op jit(solution)/shard_map/all_to_all | solution.py:27
  31.2 18.6 %copy-start.1 = (bf16[1,224,2048]{2,1,0:T(8,128)(2,1)S(1)}, bf16[1,224,2048]{2,1,0:T(8,128)(2,1)}, u32[]{:S(2)}) copy-start(bf16[1,224,2048]{2,1,0:T(8,128)(2,1)} %param.4) | copy-start | bytes 2752516
  31.2 18.6 %copy-start.2 = (bf16[1,224,2048]{2,1,0:T(8,128)(2,1)S(1)}, bf16[1,224,2048]{2,1,0:T(8,128)(2,1)}, u32[]{:S(2)}) copy-start(bf16[1,224,2048]{2,1,0:T(8,128)(2,1)} %param.3) | copy-start | bytes 2752516
  33.0 10.8 %collective-permute-start = (bf16[224,512]{1,0:T(8,128)(2,1)S(1)}, bf16[224,512]{1,0:T(8,128)(2,1)S(1)}, u32[]{:S(2)}, u32[]{:S(2)}) collective-permute-start(bf16[224,512]{1,0:T(8,128)(2,1)S(1)} %get-tuple-element.25), channel_id=1, source_target_pairs={{0,256},{256,512},{512,768},{768,0},{1,257},{257,513},{513,769},{7... | collective-permute-start | bytes 688136 | tf_op jit(solution)/shard_map/ppermute | solution.py:120
  36.2 11.9 %collective-permute-start.1 = (bf16[224,512]{1,0:T(8,128)(2,1)S(1)}, bf16[224,512]{1,0:T(8,128)(2,1)S(1)}, u32[]{:S(2)}, u32[]{:S(2)}) collective-permute-start(bf16[224,512]{1,0:T(8,128)(2,1)S(1)} %get-tuple-element.26), channel_id=1, source_target_pairs={{0,512},{256,768},{512,0},{768,256},{1,513},{257,769},{513,1},{769... | collective-permute-start | bytes 688136 | tf_op jit(solution)/shard_map/ppermute | solution.py:120
  40.7 9.1 %collective-permute-start.2 = (bf16[224,512]{1,0:T(8,128)(2,1)S(1)}, bf16[224,512]{1,0:T(8,128)(2,1)S(1)}, u32[]{:S(2)}, u32[]{:S(2)}) collective-permute-start(bf16[224,512]{1,0:T(8,128)(2,1)S(1)} %get-tuple-element.27), channel_id=1, source_target_pairs={{0,768},{256,0},{512,256},{768,512},{1,769},{257,1},{513,257},{769... | collective-permute-start | bytes 688136 | tf_op jit(solution)/shard_map/ppermute | solution.py:120
  162.6 10.3 %all-to-all-start.8 = ((f32[8,1,128]{2,1,0:T(1,128)}), f32[8,1,128]{2,1,0:T(1,128)S(1)}, u32[]{:S(2)}, u32[]{:S(2)}) async-start(f32[8,1,128]{2,1,0:T(1,128)} %broadcast_in_dim.63), calls=%async_computation.8 | async-start | bytes 8192 | tf_op jit(solution)/shard_map/all_to_all | solution.py:27
  168.4 4.7 %collective-permute-start.3 = (bf16[4,2,64,512]{3,2,1,0:T(8,128)(2,1)S(1)}, bf16[4,2,64,512]{3,2,1,0:T(8,128)(2,1)S(1)}, u32[]{:S(2)}, u32[]{:S(2)}) collective-permute-start(bf16[4,2,64,512]{3,2,1,0:T(8,128)(2,1)S(1)} %bitcast.38), channel_id=1, source_target_pairs={{0,4},{4,0},{1,5},{5,1},{2,6},{6,2},{3,7},{7,3},{8,12},{12,8},{9,1... | collective-permute-start | bytes 1572872 | tf_op jit(solution)/shard_map/ppermute | solution.py:164

commit v6 on v5

--- a/solution.py
+++ b/solution.py
@@ -137,8 +137,8 @@
     basis_h = gather(far_basis, NEAR).reshape(rank, part)
 
     left = lax.dot_general(basis_h, mean_h, (((1,), (1,)), ((), ())), preferred_element_type=f32).T
+    left = jnp.sum(gather(left.astype(bf16), "dp").astype(f32), axis=0)
     left = jnp.sum(gather(left.astype(bf16), "tensor").astype(f32), axis=0)
-    left = jnp.sum(gather(left.astype(bf16), "dp").astype(f32), axis=0)
     squares = jnp.sum(left * left, axis=0)
     left_h = left.astype(bf16)
 

time: 176 us -> 176 us (level)
  no operation moved by 1% of the time
where the time goes in v6:
time: 176 us
  blocking collectives  110 us (62%)
  starting transfers between devices  47.7 us (27%)
  waiting for transfers between devices  8.52 us (5%)
  local copies, waits for them, and re-layouts  2.65 us (2%)
  other arithmetic  2.62 us (1%)
  Pallas kernels  2.57 us (1%)
    all_to_all x7, blocking collectives, exchange(): lax.all_to_all(blocks, axes, 0, 0, axis_index_groups=groups, tiled=False)  110 us
    all_to_all x2, starting transfers between devices, exchange(): lax.all_to_all(blocks, axes, 0, 0, axis_index_groups=groups, tiled=False)  35 us
    ppermute x3, starting transfers between devices, body(): lax.ppermute(column_block((me + k) % replicas), 'dp', [(i, (i + k) % repl...  10.7 us
    ppermute x3, waiting for transfers between devices, body(): lax.ppermute(column_block((me + k) % replicas), 'dp', [(i, (i + k) % repl...  6.05 us
  transfers between devices with their start and end apart: 6, of which 3 were waited for; matrix products, arithmetic and copies ran while one was open for 1% of the time, Pallas kernels for 0%

profile of v6, /device:TPU:1, one launch (start us, length us, event | category | flops | bytes accessed | tf_op | source)
XLA Modules:
  0.0 175.7 jit_solution(8961345047128555404)
XLA Ops:
  0.6 0.0 copy-start
  0.7 0.7 copy-done
  1.4 0.7 broadcast_in_dim.25
  2.1 29.2 %all-to-all-start = ((bf16[16,4,512]{2,1,0:T(4,128)(2,1)}), bf16[16,4,512]{2,1,0:T(4,128)(2,1)S(1)}, u32[]{:S(2)}, u32[]{:S(2)}) async-start(bf16[16,4,512]{2,1,0:T(4,128)(2,1)} %broadcast_in_dim.25), calls=%async_computation | async-start | bytes 131072 | tf_op jit(solution)/shard_map/all_to_all | solution.py:27
  31.2 0.0 copy-start.1
  31.2 0.0 copy-start.2
  31.3 1.7 fusion.5
  33.0 3.2 %collective-permute-start = (bf16[224,512]{1,0:T(8,128)(2,1)S(1)}, bf16[224,512]{1,0:T(8,128)(2,1)S(1)}, u32[]{:S(2)}, u32[]{:S(2)}) collective-permute-start(bf16[224,512]{1,0:T(8,128)(2,1)S(1)} %get-tuple-element.25), channel_id=1, source_target_pairs={{0,256},{256,512},{512,768},{768,0},{1,257},{257,513},{513,769},{7... | collective-permute-start | bytes 688136 | tf_op jit(solution)/shard_map/ppermute | solution.py:120
  36.2 4.5 %collective-permute-start.1 = (bf16[224,512]{1,0:T(8,128)(2,1)S(1)}, bf16[224,512]{1,0:T(8,128)(2,1)S(1)}, u32[]{:S(2)}, u32[]{:S(2)}) collective-permute-start(bf16[224,512]{1,0:T(8,128)(2,1)S(1)} %get-tuple-element.26), channel_id=1, source_target_pairs={{0,512},{256,768},{512,0},{768,256},{1,513},{257,769},{513,1},{769... | collective-permute-start | bytes 688136 | tf_op jit(solution)/shard_map/ppermute | solution.py:120
  40.7 3.0 %collective-permute-start.2 = (bf16[224,512]{1,0:T(8,128)(2,1)S(1)}, bf16[224,512]{1,0:T(8,128)(2,1)S(1)}, u32[]{:S(2)}, u32[]{:S(2)}) collective-permute-start(bf16[224,512]{1,0:T(8,128)(2,1)S(1)} %get-tuple-element.27), channel_id=1, source_target_pairs={{0,768},{256,0},{512,256},{768,512},{1,769},{257,1},{513,257},{769... | collective-permute-start | bytes 688136 | tf_op jit(solution)/shard_map/ppermute | solution.py:120
  43.8 0.0 collective-permute-done
  43.8 4.3 %collective-permute-done.1 = bf16[224,512]{1,0:T(8,128)(2,1)S(1)} collective-permute-done((bf16[224,512]{1,0:T(8,128)(2,1)S(1)}, bf16[224,512]{1,0:T(8,128)(2,1)S(1)}, u32[]{:S(2)}, u32[]{:S(2)}) %collective-permute-start.1) | collective-permute-done | bytes 229408 | tf_op jit(solution)/shard_map/ppermute | solution.py:120
  48.1 1.7 collective-permute-done.2
  49.8 0.0 copy-done.1
  49.8 0.0 copy-done.2
  49.8 0.2 fusion.3
  50.0 0.0 all-to-all-done
  50.1 9.2 %all_to_all.45 = bf16[4,64,512]{2,1,0:T(8,128)(2,1)S(1)} all-to-all(bf16[4,64,512]{2,1,0:T(8,128)(2,1)S(1)} %broadcast_in_dim.26), channel_id=1, replica_groups=mesh['dp'=4,'zh'=16,'zl'=2,'core'=2,'tensor'=4] {'core','zl'}, dimensions={0} | all-to-all | bytes 524288 | tf_op jit(solution)/shard_map/all_to_all | solution.py:27
  59.2 0.2 convolution_convert_fusion.1
  59.5 11.4 %all_to_all.46 = bf16[4,224,256]{2,1,0:T(8,128)(2,1)S(1)} all-to-all(bf16[4,224,256]{2,1,0:T(8,128)(2,1)S(1)} %broadcast_in_dim.27), channel_id=1, replica_groups=mesh['dp'=4,'zh'=16,'zl'=2,'core'=2,'tensor'=4] {'dp'}, dimensions={0} | all-to-all | bytes 917504 | tf_op jit(solution)/shard_map/all_to_all | solution.py:27
  71.0 0.1 reduce_sum.96
  71.1 10.4 %all_to_all.47 = bf16[4,224,256]{2,1,0:T(8,128)(2,1)S(1)} all-to-all(bf16[4,224,256]{2,1,0:T(8,128)(2,1)S(1)} %broadcast_in_dim.28), channel_id=1, replica_groups=mesh['dp'=4,'zh'=16,'zl'=2,'core'=2,'tensor'=4] {'tensor'}, dimensions={0} | all-to-all | bytes 917504 | tf_op jit(solution)/shard_map/all_to_all | solution.py:27
  81.5 0.1 convert_reduce_fusion
  81.6 0.2 convolution_convert_fusion
  81.9 12.0 %all_to_all.48 = bf16[4,64,640]{2,1,0:T(8,128)(2,1)S(1)} all-to-all(bf16[4,64,640]{2,1,0:T(8,128)(2,1)S(1)} %pad_maximum_fusion), channel_id=1, replica_groups=mesh['dp'=4,'zh'=16,'zl'=2,'core'=2,'tensor'=4] {'core','zl'}, dimensions={0} | all-to-all | bytes 655360 | tf_op jit(solution)/shard_map/all_to_all | solution.py:27
  94.1 28.4 %all_to_all.49 = bf16[16,4,640]{2,1,0:T(4,128)(2,1)S(1)} all-to-all(bf16[16,4,640]{2,1,0:T(4,128)(2,1)S(1)} %pad_maximum_fusion.1), channel_id=1, replica_groups={{80,96,112,128,144,160,176,192,208,224,240,0,16,32,48,64},{81,97,113,12..., dimensions={0} | all-to-all | bytes 163840 | tf_op jit(solution)/shard_map/all_to_all | solution.py:27
  122.6 0.1 dynamic_slice.45
  122.7 0.1 divide_convert_fusion
  122.8 27.8 %all_to_all.50 = bf16[16,4,512]{2,1,0:T(4,128)(2,1)S(1)} all-to-all(bf16[16,4,512]{2,1,0:T(4,128)(2,1)S(1)} %broadcast_in_dim.29), channel_id=1, replica_groups={{80,96,112,128,144,160,176,192,208,224,240,0,16,32,48,64},{81,97,113,12..., dimensions={0} | all-to-all | bytes 131072 | tf_op jit(solution)/shard_map/all_to_all | solution.py:27
  150.7 11.0 %all_to_all.51 = bf16[8,64,512]{2,1,0:T(8,128)(2,1)S(1)} all-to-all(bf16[8,64,512]{2,1,0:T(8,128)(2,1)S(1)} %broadcast_in_dim.61), channel_id=1, replica_groups=mesh['dp'=4,'zh'=16,'zl'=2,'core'=2,'tensor'=4] {'dp','zl'}, dimensions={0} | all-to-all | bytes 1048576 | tf_op jit(solution)/shard_map/all_to_all | solution.py:27
  161.7 0.2 multiply_reduce_fusion
  161.9 0.1 broadcast_in_dim.62
  162.0 0.6 broadcast_in_dim.63
  162.6 5.8 %all-to-all-start.8 = ((f32[8,1,128]{2,1,0:T(1,128)}), f32[8,1,128]{2,1,0:T(1,128)S(1)}, u32[]{:S(2)}, u32[]{:S(2)}) async-start(f32[8,1,128]{2,1,0:T(1,128)} %broadcast_in_dim.63), calls=%async_computation.8 | async-start | bytes 8192 | tf_op jit(solution)/shard_map/all_to_all | solution.py:27
  168.4 2.0 %collective-permute-start.3 = (bf16[4,2,64,512]{3,2,1,0:T(8,128)(2,1)S(1)}, bf16[4,2,64,512]{3,2,1,0:T(8,128)(2,1)S(1)}, u32[]{:S(2)}, u32[]{:S(2)}) collective-permute-start(bf16[4,2,64,512]{3,2,1,0:T(8,128)(2,1)S(1)} %bitcast.38), channel_id=1, source_target_pairs={{0,4},{4,0},{1,5},{5,1},{2,6},{6,2},{3,7},{7,3},{8,12},{12,8},{9,1... | collective-permute-start | bytes 1572872 | tf_op jit(solution)/shard_map/ppermute | solution.py:164
  170.4 2.5 %all-to-all-done.8 = f32[8,1,128]{2,1,0:T(1,128)S(1)} async-done(((f32[8,1,128]{2,1,0:T(1,128)}), f32[8,1,128]{2,1,0:T(1,128)S(1)}, u32[]{:S(2)}, u32[]{:S(2)}) %all-to-all-start.8) | async-done | bytes 4128 | tf_op jit(solution)/shard_map/all_to_all | solution.py:27
  172.9 0.1 dynamic-slice_bitcast_fusion.1
  173.0 0.1 copy.22.own_norms_ref
  173.1 0.0 collective-permute-done.3.other_ref
  173.1 2.6 %shard_map.58 = (bf16[224,2048]{1,0:T(8,128)(2,1)}, bf16[224,2048]{1,0:T(8,128)(2,1)}, f32[4,2048]{1,0:T(4,128)}) custom-call(s32[1]{0:T(128)} %bitcast.core_ref, bf16[224,256]{1,0:T(8,128)(2,1)S(1)} %get-tuple-element.29.left_ref, f32[2,256]{1,0:T(2,128)S(1)} %pad_maximum_fusion.2.norms_ref, bf16[4,2,64,512]{3,2,1,0:T(8,128)(2,1)S(1)} %bitcast.40, ...), custom_call_target="tpu_custom_call" | custom-call | tf_op jit(solution)/shard_map/pallas_call | solution.py:78
  (31 shorter events, 0.6 us)
Async XLA Ops:
  0.6 0.8 copy-start
  2.1 48.0 %all-to-all-start = ((bf16[16,4,512]{2,1,0:T(4,128)(2,1)}), bf16[16,4,512]{2,1,0:T(4,128)(2,1)S(1)}, u32[]{:S(2)}, u32[]{:S(2)}) async-start(bf16[16,4,512]{2,1,0:T(4,128)(2,1)} %broadcast_in_dim.25), calls=%async_computation | async-start | bytes 131072 | tf_op jit(solution)/shard_map/all_to_all | solution.py:27
  31.2 18.6 %copy-start.1 = (bf16[1,224,2048]{2,1,0:T(8,128)(2,1)S(1)}, bf16[1,224,2048]{2,1,0:T(8,128)(2,1)}, u32[]{:S(2)}) copy-start(bf16[1,224,2048]{2,1,0:T(8,128)(2,1)} %param.4) | copy-start | bytes 2752516
  31.2 18.6 %copy-start.2 = (bf16[1,224,2048]{2,1,0:T(8,128)(2,1)S(1)}, bf16[1,224,2048]{2,1,0:T(8,128)(2,1)}, u32[]{:S(2)}) copy-start(bf16[1,224,2048]{2,1,0:T(8,128)(2,1)} %param.3) | copy-start | bytes 2752516
  33.0 10.8 %collective-permute-start = (bf16[224,512]{1,0:T(8,128)(2,1)S(1)}, bf16[224,512]{1,0:T(8,128)(2,1)S(1)}, u32[]{:S(2)}, u32[]{:S(2)}) collective-permute-start(bf16[224,512]{1,0:T(8,128)(2,1)S(1)} %get-tuple-element.25), channel_id=1, source_target_pairs={{0,256},{256,512},{512,768},{768,0},{1,257},{257,513},{513,769},{7... | collective-permute-start | bytes 688136 | tf_op jit(solution)/shard_map/ppermute | solution.py:120
  36.2 11.9 %collective-permute-start.1 = (bf16[224,512]{1,0:T(8,128)(2,1)S(1)}, bf16[224,512]{1,0:T(8,128)(2,1)S(1)}, u32[]{:S(2)}, u32[]{:S(2)}) collective-permute-start(bf16[224,512]{1,0:T(8,128)(2,1)S(1)} %get-tuple-element.26), channel_id=1, source_target_pairs={{0,512},{256,768},{512,0},{768,256},{1,513},{257,769},{513,1},{769... | collective-permute-start | bytes 688136 | tf_op jit(solution)/shard_map/ppermute | solution.py:120
  40.7 9.1 %collective-permute-start.2 = (bf16[224,512]{1,0:T(8,128)(2,1)S(1)}, bf16[224,512]{1,0:T(8,128)(2,1)S(1)}, u32[]{:S(2)}, u32[]{:S(2)}) collective-permute-start(bf16[224,512]{1,0:T(8,128)(2,1)S(1)} %get-tuple-element.27), channel_id=1, source_target_pairs={{0,768},{256,0},{512,256},{768,512},{1,769},{257,1},{513,257},{769... | collective-permute-start | bytes 688136 | tf_op jit(solution)/shard_map/ppermute | solution.py:120
  162.6 10.3 %all-to-all-start.8 = ((f32[8,1,128]{2,1,0:T(1,128)}), f32[8,1,128]{2,1,0:T(1,128)S(1)}, u32[]{:S(2)}, u32[]{:S(2)}) async-start(f32[8,1,128]{2,1,0:T(1,128)} %broadcast_in_dim.63), calls=%async_computation.8 | async-start | bytes 8192 | tf_op jit(solution)/shard_map/all_to_all | solution.py:27
  168.4 4.7 %collective-permute-start.3 = (bf16[4,2,64,512]{3,2,1,0:T(8,128)(2,1)S(1)}, bf16[4,2,64,512]{3,2,1,0:T(8,128)(2,1)S(1)}, u32[]{:S(2)}, u32[]{:S(2)}) collective-permute-start(bf16[4,2,64,512]{3,2,1,0:T(8,128)(2,1)S(1)} %bitcast.38), channel_id=1, source_target_pairs={{0,4},{4,0},{1,5},{5,1},{2,6},{6,2},{3,7},{7,3},{8,12},{12,8},{9,1... | collective-permute-start | bytes 1572872 | tf_op jit(solution)/shard_map/ppermute | solution.py:164
